TPU v7x, 128 devices: a whole 4x4x4 slice. The times are simulated.
128 devices in a mesh: rep: 8 (over y, x_lo), fsdp: 16 (over z, x_hi, core).
Axes of the slice: x: 4 (x_hi: 2, x_lo: 2; x = x_hi * 2 + x_lo), y: 4, z: 4, core: 2. Of those that a mesh axis runs over, the one named last changes fastest.
Arguments:
- tokens: bfloat16 [16384, 1152], P(('rep', 'fsdp')), may hold values from -6 to 6
- lengths: int32 [8, 4], P('rep'), may hold values from 1 to 1536, 2048 in all within a row
- cotangent: bfloat16 [16384, 1152], P(('rep', 'fsdp')), may hold values from -6 to 6
- pre_attention: bfloat16 [1152], P('fsdp'), may hold values from 0.5 to 1.5
- post_attention: bfloat16 [1152], P('fsdp'), may hold values from 0.5 to 1.5
- pre_forward: bfloat16 [1152], P('fsdp'), may hold values from 0.5 to 1.5
- post_forward: bfloat16 [1152], P('fsdp'), may hold values from 0.5 to 1.5
- query_gain: bfloat16 [256], P('fsdp'), may hold values from 0.5 to 1.5
- key_gain: bfloat16 [256], P('fsdp'), may hold values from 0.5 to 1.5
- query_weight: bfloat16 [1152, 1024], P('fsdp'), may hold values from -0.1875 to 0.1875
- key_weight: bfloat16 [1152, 256], P('fsdp'), may hold values from -0.1875 to 0.1875
- value_weight: bfloat16 [1152, 256], P('fsdp'), may hold values from -0.1875 to 0.1875
- output_weight: bfloat16 [1024, 1152], P('fsdp'), may hold values from -0.1875 to 0.1875
- gate_rows: bfloat16 [6912, 1152], P('fsdp'), may hold values from -0.1875 to 0.1875
- up_rows: bfloat16 [6912, 1152], P('fsdp'), may hold values from -0.1875 to 0.1875
- down_rows: bfloat16 [6912, 1152], P('fsdp'), may hold values from -0.078125 to 0.078125
Outputs:
- output: bfloat16 [16384, 1152], P(('rep', 'fsdp'))
- grad_tokens: float32 [16384, 1152], P(('rep', 'fsdp'))
- grad_pre_attention: float32 [1152], P('fsdp')
- grad_post_attention: float32 [1152], P('fsdp')
- grad_pre_forward: float32 [1152], P('fsdp')
- grad_post_forward: float32 [1152], P('fsdp')
- grad_query_gain: float32 [256], P('fsdp')
- grad_key_gain: float32 [256], P('fsdp')
- grad_query_weight: float32 [1152, 1024], P('fsdp')
- grad_key_weight: float32 [1152, 256], P('fsdp')
- grad_value_weight: float32 [1152, 256], P('fsdp')
- grad_output_weight: float32 [1024, 1152], P('fsdp')
- grad_gate_rows: float32 [6912, 1152], P('fsdp')
- grad_up_rows: float32 [6912, 1152], P('fsdp')
- grad_down_rows: float32 [6912, 1152], P('fsdp')
Inputs may be any that keep to these rules, and one draw needn't show every extreme that they name: Each row lists the lengths of 4 documents that fill one replica group's 2048 tokens in order; a row sums to 2048 and its longest document has exactly 1536 tokens.
All inputs are finite; a program needn't handle non-finite values.
Results may differ from a plain program's by a relative error of at most 0.028.
Values may be sent and summed in bfloat16 or wider, within the bound.
No kernel may reach another device: no remote copies, remote signals or barrier semaphores. Data moves between devices by JAX's collectives and lax.ppermute only.
A program may use at most 128 MiB of HBM per device.

v0:
```python
import jax
import jax.numpy as jnp
from jax import lax
from jax.sharding import PartitionSpec as P

WINDOW = 512


EPSILON = 1e-06
MASKED = -1e30
CONTRACT_LAST = (((1,), (1,)), ((), ()))
CONTRACT_FIRST = (((0,), (0,)), ((), ()))


def sent_together(arrays, axis, dim, along):
    widths = [a.shape[along] for a in arrays]
    both = jnp.concatenate(arrays, axis=along)
    whole = lax.all_gather(both, axis, axis=dim, tiled=True)
    return tuple(jnp.split(whole, [sum(widths[:k]) for k in range(1, len(widths))], axis=along))


def shifted(block, axis, distance):
    devices = range(lax.axis_size(axis))
    route = [(i - distance, i) for i in devices if i - distance in devices]
    return lax.ppermute(block, axis, route)


def sent_together_2(arrays, axis, dim, along):
    ends, at = ([], 0)
    for a in arrays[:-1]:
        at += a.shape[along]
        ends.append(at)
    both = jnp.concatenate(arrays, axis=along)
    return tuple(
        jnp.split(lax.psum_scatter(both, axis, scatter_dimension=dim, tiled=True), ends, axis=along)
    )


def from_everyone(x, axis):
    copies = jnp.broadcast_to(x, (lax.axis_size(axis), *x.shape))
    return lax.all_to_all(copies, axis, split_axis=0, concat_axis=0, tiled=True)


def taken_together(x, axis):
    everything = from_everyone(x, axis)
    return jnp.sum(everything.astype(jnp.float32), axis=0)


def rows_for(lines, devices):
    spare = -len(lines) % devices
    return jnp.pad(lines, [(0, spare)] + [(0, 0)] * (lines.ndim - 1))


def sum_by_parts(x, axis):
    lines = x.reshape(-1, *x.shape[1:][-1:])
    own = lax.psum_scatter(
        rows_for(lines, lax.axis_size(axis)), axis, scatter_dimension=0, tiled=True
    )
    whole = lax.all_gather(own, axis).reshape(-1, *lines.shape[1:])
    return lax.slice_in_dim(whole, 0, len(lines)).reshape(x.shape)


def norm_rows(values, gain):
    return values * lax.rsqrt(jnp.mean(values * values, axis=-1, keepdims=True) + EPSILON) * gain


def rotate(values, position):
    half = values.shape[-1] // 2
    freq = 10000.0 ** (-2.0 * jnp.arange(half, dtype=jnp.float32) / values.shape[-1])
    angle = position.astype(jnp.float32)[:, None] * freq[None, :]
    cosine = jnp.cos(angle)[:, None, :]
    sine = jnp.sin(angle)[:, None, :]
    first = values[..., :half]
    second = values[..., half:]
    return jnp.concatenate(
        [first * cosine - second * sine, second * cosine + first * sine], axis=-1
    )


def doc_info(lengths, index):
    ends = jnp.cumsum(lengths)
    starts = ends - lengths
    segment = jnp.sum((index[:, None] >= ends[None, :-1]).astype(jnp.int32), axis=1)
    hit = segment[:, None] == jnp.arange(lengths.shape[0], dtype=jnp.int32)[None, :]
    first = jnp.sum(jnp.where(hit, starts[None, :], 0), axis=1)
    segment = jnp.where(index < 0, -1, segment)
    return (segment, index - first)


def activate(gate, upward):
    return jax.nn.gelu(gate, approximate=True) * upward


def local(
    tokens,
    lengths,
    cotangent,
    pre_attention,
    post_attention,
    pre_forward,
    post_forward,
    query_gain,
    key_gain,
    query_weight,
    key_weight,
    value_weight,
    output_weight,
    gate_rows,
    up_rows,
    down_rows,
):
    rows = tokens.shape[0]
    width = tokens.shape[1]
    head_size = key_weight.shape[1]
    heads = query_weight.shape[1] // head_size
    blocks_back = (WINDOW + rows - 1) // rows
    shard = lax.axis_index("fsdp")
    local_index = shard * rows + jnp.arange(rows, dtype=jnp.int32)
    key_index = (shard - blocks_back) * rows + jnp.arange(rows * (blocks_back + 1), dtype=jnp.int32)
    query_seg, query_pos = doc_info(lengths[0], local_index)
    key_seg, key_place = doc_info(lengths[0], key_index)
    distance = local_index[:, None] - key_index[None, :]
    allowed = (query_seg[:, None] == key_seg[None, :]) & (distance >= 0) & (distance < WINDOW)
    gathered = (
        lax.all_gather(pre_attention, "fsdp", axis=0, tiled=True),
        lax.all_gather(post_attention, "fsdp", axis=0, tiled=True),
        lax.all_gather(pre_forward, "fsdp", axis=0, tiled=True),
        lax.all_gather(post_forward, "fsdp", axis=0, tiled=True),
        lax.all_gather(query_gain, "fsdp", axis=0, tiled=True),
        lax.all_gather(key_gain, "fsdp", axis=0, tiled=True),
        *sent_together((query_weight, key_weight, value_weight), "fsdp", 0, 1),
        lax.all_gather(output_weight, "fsdp", axis=0, tiled=True),
    )
    gain_pre_att = gathered[0].astype(jnp.float32)
    gain_post_att = gathered[1].astype(jnp.float32)
    gain_pre_fwd = gathered[2].astype(jnp.float32)
    gain_post_fwd = gathered[3].astype(jnp.float32)
    gain_query = gathered[4].astype(jnp.float32)
    gain_key = gathered[5].astype(jnp.float32)
    weight_query, weight_key, weight_value, weight_output = (
        gathered[6],
        gathered[7],
        gathered[8],
        gathered[9],
    )
    inputs = tokens.astype(jnp.float32)
    normed_one, pull_one = jax.vjp(norm_rows, inputs, gain_pre_att)
    normed_low = normed_one.astype(jnp.bfloat16)
    query_lin = jnp.dot(normed_low, weight_query, preferred_element_type=jnp.float32)
    key_lin = jnp.dot(normed_low, weight_key, preferred_element_type=jnp.float32)
    value_low = jnp.dot(normed_low, weight_value, preferred_element_type=jnp.float32).astype(
        jnp.bfloat16
    )

    def query_side(lin, gain):
        return rotate(
            norm_rows(lin.reshape(rows, heads, head_size), gain), query_pos
        ) * head_size ** (-0.5)

    def key_side(lin, gain):
        return rotate(norm_rows(lin[:, None, :], gain), query_pos)[:, 0, :]

    query_value, pull_query = jax.vjp(query_side, query_lin, gain_query)
    key_value, pull_key = jax.vjp(key_side, key_lin, gain_key)
    query_low = query_value.astype(jnp.bfloat16)
    key_low = key_value.astype(jnp.bfloat16)
    outgoing = jnp.concatenate([key_low, value_low], axis=1)
    arrived = []
    for step in range(blocks_back, 0, -1):
        arrived.append(shifted(outgoing, "fsdp", step))
    both = jnp.concatenate(arrived + [outgoing], axis=0)
    keys_all = both[:, :head_size]
    values_all = both[:, head_size:]
    scores = jnp.einsum("thd,kd->htk", query_low, keys_all, preferred_element_type=jnp.float32)
    scores = jnp.where(allowed[None], scores, MASKED)
    peak = jnp.max(scores, axis=-1, keepdims=True)
    expo = jnp.exp(scores - peak)
    total = jnp.sum(expo, axis=-1, keepdims=True)
    log_total = peak + jnp.log(total)
    probs_low = (expo / total).astype(jnp.bfloat16)
    mixed = jnp.einsum("htk,kd->thd", probs_low, values_all, preferred_element_type=jnp.float32)
    mixed_low = mixed.reshape(rows, heads * head_size).astype(jnp.bfloat16)
    projected = jnp.dot(mixed_low, weight_output, preferred_element_type=jnp.float32)
    attended, pull_two = jax.vjp(norm_rows, projected, gain_post_att)
    residual_one = inputs + attended
    normed_two, pull_three = jax.vjp(norm_rows, residual_one, gain_pre_fwd)
    normed_two_low = normed_two.astype(jnp.bfloat16)
    group_normed = lax.all_gather(normed_two_low, "fsdp", axis=0, tiled=True)
    gate = lax.dot_general(
        group_normed, gate_rows, CONTRACT_LAST, preferred_element_type=jnp.float32
    )
    upward = lax.dot_general(
        group_normed, up_rows, CONTRACT_LAST, preferred_element_type=jnp.float32
    )
    hidden = activate(gate, upward).astype(jnp.bfloat16)
    down_sum = lax.psum_scatter(
        jnp.dot(hidden, down_rows, preferred_element_type=jnp.float32).astype(jnp.bfloat16),
        "fsdp",
        scatter_dimension=0,
        tiled=True,
    ).astype(jnp.float32)
    fed, pull_four = jax.vjp(norm_rows, down_sum, gain_post_fwd)
    output = (residual_one + fed).astype(jnp.bfloat16)
    grad_out = cotangent.astype(jnp.float32)
    grad_down, grad_post_fwd = pull_four(grad_out)
    grad_down_low = grad_down.astype(jnp.bfloat16)
    group_grad_down = lax.all_gather(grad_down_low, "fsdp", axis=0, tiled=True)
    group_gate = lax.dot_general(
        group_normed, gate_rows, CONTRACT_LAST, preferred_element_type=jnp.float32
    )
    group_up = lax.dot_general(
        group_normed, up_rows, CONTRACT_LAST, preferred_element_type=jnp.float32
    )
    group_hidden, pull_group = jax.vjp(activate, group_gate, group_up)
    group_grad_hidden = lax.dot_general(
        group_grad_down, down_rows, CONTRACT_LAST, preferred_element_type=jnp.float32
    )
    group_grad_gate, group_grad_up = pull_group(group_grad_hidden)
    group_gate_low = group_grad_gate.astype(jnp.bfloat16)
    group_up_low = group_grad_up.astype(jnp.bfloat16)
    group_hidden_low = group_hidden.astype(jnp.bfloat16)
    grad_normed_two = lax.psum_scatter(
        (
            jnp.dot(group_gate_low, gate_rows, preferred_element_type=jnp.float32)
            + jnp.dot(group_up_low, up_rows, preferred_element_type=jnp.float32)
        ).astype(jnp.bfloat16),
        "fsdp",
        scatter_dimension=0,
        tiled=True,
    ).astype(jnp.float32)
    group_row_grads = jnp.concatenate(
        [
            lax.dot_general(
                group_gate_low, group_normed, CONTRACT_FIRST, preferred_element_type=jnp.float32
            ),
            lax.dot_general(
                group_up_low, group_normed, CONTRACT_FIRST, preferred_element_type=jnp.float32
            ),
            lax.dot_general(
                group_hidden_low,
                group_grad_down,
                CONTRACT_FIRST,
                preferred_element_type=jnp.float32,
            ),
        ],
        axis=1,
    )
    extra_three, grad_pre_fwd = pull_three(grad_normed_two)
    grad_residual = grad_out + extra_three
    grad_projected, grad_post_att = pull_two(grad_residual)
    grad_proj_low = grad_projected.astype(jnp.bfloat16)
    back_set = (weight_query, weight_key, weight_value, weight_output)
    back_query, back_key, back_value, back_output = back_set
    grad_mixed_low = lax.dot_general(
        grad_proj_low, back_output, CONTRACT_LAST, preferred_element_type=jnp.float32
    ).astype(jnp.bfloat16)
    grad_output_weight = lax.dot_general(
        mixed_low, grad_proj_low, CONTRACT_FIRST, preferred_element_type=jnp.float32
    )
    grad_mixed_heads = grad_mixed_low.reshape(rows, heads, head_size)
    probs = jnp.exp(scores - log_total)
    probs_again = probs.astype(jnp.bfloat16)
    grad_probs = jnp.einsum(
        "thd,kd->htk", grad_mixed_heads, values_all, preferred_element_type=jnp.float32
    )
    inner = jnp.sum(grad_probs * probs, axis=-1, keepdims=True)
    grad_scores = (probs * (grad_probs - inner)).astype(jnp.bfloat16)
    grad_query_low = jnp.einsum(
        "htk,kd->thd", grad_scores, keys_all, preferred_element_type=jnp.float32
    ).astype(jnp.bfloat16)
    grad_keys_all = jnp.einsum(
        "htk,thd->kd", grad_scores, query_low, preferred_element_type=jnp.float32
    )
    grad_values_all = jnp.einsum(
        "htk,thd->kd", probs_again, grad_mixed_heads, preferred_element_type=jnp.float32
    )
    grad_both = jnp.concatenate([grad_keys_all, grad_values_all], axis=1)
    owned_both = grad_both[blocks_back * rows :]
    for step in range(1, blocks_back + 1):
        piece = grad_both[(blocks_back - step) * rows : (blocks_back - step + 1) * rows]
        owned_both = owned_both + shifted(piece.astype(jnp.bfloat16), "fsdp", -step).astype(
            piece.dtype
        )
    grad_key_low = owned_both[:, :head_size].astype(jnp.bfloat16)
    grad_value_low = owned_both[:, head_size:].astype(jnp.bfloat16)
    grad_query_lin, grad_query_gain = pull_query(grad_query_low.astype(jnp.float32))
    grad_key_lin, grad_key_gain = pull_key(grad_key_low.astype(jnp.float32))
    query_lin_low = grad_query_lin.astype(jnp.bfloat16)
    key_lin_low = grad_key_lin.astype(jnp.bfloat16)
    grad_normed_one = (
        lax.dot_general(
            query_lin_low, back_query, CONTRACT_LAST, preferred_element_type=jnp.float32
        )
        + lax.dot_general(key_lin_low, back_key, CONTRACT_LAST, preferred_element_type=jnp.float32)
        + lax.dot_general(
            grad_value_low, back_value, CONTRACT_LAST, preferred_element_type=jnp.float32
        )
    )
    grad_query_weight = lax.dot_general(
        normed_low, query_lin_low, CONTRACT_FIRST, preferred_element_type=jnp.float32
    )
    grad_key_weight = lax.dot_general(
        normed_low, key_lin_low, CONTRACT_FIRST, preferred_element_type=jnp.float32
    )
    grad_value_weight = lax.dot_general(
        normed_low, grad_value_low, CONTRACT_FIRST, preferred_element_type=jnp.float32
    )
    extra_one, grad_pre_att = pull_one(grad_normed_one)
    grad_inputs = grad_residual + extra_one
    owned = (
        lax.psum_scatter(
            grad_pre_att.astype(jnp.bfloat16), "fsdp", scatter_dimension=0, tiled=True
        ).astype(jnp.float32),
        lax.psum_scatter(
            grad_post_att.astype(jnp.bfloat16), "fsdp", scatter_dimension=0, tiled=True
        ).astype(jnp.float32),
        lax.psum_scatter(
            grad_pre_fwd.astype(jnp.bfloat16), "fsdp", scatter_dimension=0, tiled=True
        ).astype(jnp.float32),
        lax.psum_scatter(
            grad_post_fwd.astype(jnp.bfloat16), "fsdp", scatter_dimension=0, tiled=True
        ).astype(jnp.float32),
        lax.psum_scatter(
            grad_query_gain.astype(jnp.bfloat16), "fsdp", scatter_dimension=0, tiled=True
        ).astype(jnp.float32),
        lax.psum_scatter(
            grad_key_gain.astype(jnp.bfloat16), "fsdp", scatter_dimension=0, tiled=True
        ).astype(jnp.float32),
        *tuple(
            (
                part.astype(jnp.float32)
                for part in sent_together_2(
                    (
                        grad_query_weight.astype(jnp.bfloat16),
                        grad_key_weight.astype(jnp.bfloat16),
                        grad_value_weight.astype(jnp.bfloat16),
                    ),
                    "fsdp",
                    0,
                    1,
                )
            )
        ),
        lax.psum_scatter(
            grad_output_weight.astype(jnp.bfloat16), "fsdp", scatter_dimension=0, tiled=True
        ).astype(jnp.float32),
    )
    owned = (
        taken_together(owned[0].astype(jnp.bfloat16), "rep").astype(jnp.float32),
        taken_together(owned[1].astype(jnp.bfloat16), "rep").astype(jnp.float32),
        taken_together(owned[2].astype(jnp.bfloat16), "rep").astype(jnp.float32),
        taken_together(owned[3].astype(jnp.bfloat16), "rep").astype(jnp.float32),
        taken_together(owned[4].astype(jnp.bfloat16), "rep").astype(jnp.float32),
        taken_together(owned[5].astype(jnp.bfloat16), "rep").astype(jnp.float32),
        taken_together(owned[6].astype(jnp.bfloat16), "rep").astype(jnp.float32),
        taken_together(owned[7].astype(jnp.bfloat16), "rep").astype(jnp.float32),
        taken_together(owned[8].astype(jnp.bfloat16), "rep").astype(jnp.float32),
        taken_together(owned[9].astype(jnp.bfloat16), "rep").astype(jnp.float32),
    )
    owned_rows = sum_by_parts(group_row_grads.astype(jnp.bfloat16), "rep").astype(jnp.float32)
    return (
        output,
        grad_inputs,
        owned[0],
        owned[1],
        owned[2],
        owned[3],
        owned[4],
        owned[5],
        owned[6],
        owned[7],
        owned[8],
        owned[9],
        owned_rows[:, :width],
        owned_rows[:, width : 2 * width],
        owned_rows[:, 2 * width :],
    )


def solution(mesh):
    placed = (
        P(("rep", "fsdp"), None),
        P("rep", None),
        P(("rep", "fsdp"), None),
        P("fsdp"),
        P("fsdp"),
        P("fsdp"),
        P("fsdp"),
        P("fsdp"),
        P("fsdp"),
        P("fsdp", None),
        P("fsdp", None),
        P("fsdp", None),
        P("fsdp", None),
        P("fsdp", None),
        P("fsdp", None),
        P("fsdp", None),
    )
    return jax.shard_map(
        local,
        mesh=mesh,
        in_specs=placed,
        out_specs=(
            P(("rep", "fsdp"), None),
            P(("rep", "fsdp"), None),
            P("fsdp"),
            P("fsdp"),
            P("fsdp"),
            P("fsdp"),
            P("fsdp"),
            P("fsdp"),
            P("fsdp", None),
            P("fsdp", None),
            P("fsdp", None),
            P("fsdp", None),
            P("fsdp", None),
            P("fsdp", None),
            P("fsdp", None),
        ),
        check_vma=False,
    )
```

profile of v0, /device:TPU:0, one launch (start us, length us, event | category | flops | bytes accessed | tf_op | source)
XLA Modules:
  0.0 789.1 jit_solution(8885573738614350753)
XLA Ops:
  20.8 71.2 %all-reduce.19 = (bf16[1152]{0:T(1024)(128)(2,1)S(1)}, bf16[256]{0:T(256)(128)(2,1)S(1)}, bf16[256]{0:T(256)(128)(2,1)S(1)}, bf16[1152]{0:T(1024)(128)(2,1)S(1)}...) all-reduce(bf16[1152]{0:T(1024)(128)(2,1)S(1)} %dynamic-update-slic, ...), channel_id=1, replica_groups=mesh['rep'=8,'fsdp'=16] {'fsdp'}, use_global_device_ids=true, to_apply=%add.4 | all-reduce | flops 5120 | bytes 20480
  103.5 3.7 collective-permute-done
  110.2 7.7 all-gather.10.cloned.1.call-done
  122.2 57.0 %all-gather.12.cloned.1.call-done = bf16[2048,1152]{1,0:T(8,128)(2,1)} async-done(((bf16[128,1152]{1,0:T(8,128)(2,1)}), bf16[2048,1152]{1,0:T(8,128)(2,1)}) %all-gather.12.cloned.1.call-update) | async-done | bytes 4718608 | tf_op jit(solution)/shard_map/all_gather | solution.py:188
  179.2 5.2 fusion.103
  184.5 4.6 multiply_convert_fusion.1
  190.3 4.6 convolution_convert_fusion
  195.6 80.1 %reduce-scatter.9.cloned.1.call-done = bf16[128,1152]{1,0:T(8,128)(2,1)} async-done(((bf16[2048,1152]{1,0:T(8,128)(2,1)}), bf16[128,1152]{1,0:T(8,128)(2,1)}) %reduce-scatter.9.cloned.1.call-update) | async-done | bytes 294928 | tf_op jit(solution)/shard_map/reduce_scatter | solution.py:196
  280.6 56.6 %all-gather.14.cloned.1.call-done = bf16[2048,1152]{1,0:T(8,128)(2,1)} async-done(((bf16[128,1152]{1,0:T(8,128)(2,1)}), bf16[2048,1152]{1,0:T(8,128)(2,1)}) %all-gather.14.cloned.1.call-update) | async-done | bytes 4718608 | tf_op jit(solution)/shard_map/all_gather | solution.py:207
  337.2 8.8 %multiply_convert_fusion = (bf16[2048,432]{0,1:T(8,128)(2,1)S(1)}, bf16[2048,432]{0,1:T(8,128)(2,1)S(1)}) fusion(f32[2048,432]{0,1:T(8,128)} %copy-done.60, f32[2048,432]{0,1:T(8,128)} %get-tuple-element.73, bf16[2048,1152]{1,0:T(8,128)(2,1)} %all-gather.14.cloned.1.call-done, bf16[432,1152]{1,0:T(8,128)(2,1)S(1)} %copy-done), kind=kOutput, calls=%fused_computation.14 | convolution fusion | flops 2059665408 | bytes 16330752 | tf_op jit(solution)/shard_map/dot_general | solution.py:215
  346.0 3.0 fusion.104
  349.0 4.6 add_convert_fusion
  353.9 5.4 convolution_convert_fusion.3
  359.4 5.1 convolution_convert_fusion.4
  364.6 5.1 convolution_convert_fusion.5
  371.5 62.9 %reduce-scatter.11.cloned.1.call-done = bf16[128,1152]{1,0:T(8,128)(2,1)} async-done(((bf16[2048,1152]{1,0:T(8,128)(2,1)}), bf16[128,1152]{1,0:T(8,128)(2,1)}) %reduce-scatter.11.cloned.1.call-update) | async-done | bytes 294928 | tf_op jit(solution)/shard_map/reduce_scatter | solution.py:222
  435.6 2.8 multiply_reduce_fusion.1
  441.5 82.6 %fusion = bf16[64,3456]{1,0:T(8,128)(2,1)S(1)} fusion(bf16[432,3456]{1,0:T(8,128)(2,1)} %pad_maximum_fusion.1), kind=kCustom, calls=%all-reduce-scatter | all-reduce-scatter fusion | flops 1769473 | bytes 3428864
  528.8 5.6 collective-permute-done.9
  534.4 4.2 concatenate.34
  539.5 2.6 convolution_convert_fusion.8
  554.6 3.4 collective-permute-done.7
  558.0 4.8 collective-permute-done.6
  562.8 2.4 collective-permute-done.5
  566.8 6.5 pad_maximum_fusion
  573.4 5.8 copy.204
  579.8 2.6 fusion.8
  585.4 69.6 %all-reduce.18 = (bf16[1152]{0:T(1024)(128)(2,1)S(1)}, bf16[1152]{0:T(1024)(128)(2,1)S(1)}, bf16[1152]{0:T(1024)(128)(2,1)S(1)}, bf16[1152]{0:T(1024)(128)(2,1)S...) all-reduce(bf16[1152]{0:T(1024)(128)(2,1)S(1)} %get-tuple-element.2, ...), channel_id=5, replica_groups=mesh['rep'=8,'fsdp'=16] {'fsdp'}, use_global_device_ids=true, to_apply=%region_22.23.clone | all-reduce | flops 5120 | bytes 20480
  655.7 5.1 all-to-all-start.4
  660.9 6.0 all-to-all-done.4
  667.5 3.3 all-to-all-start.5
  671.6 5.3 all-to-all-done.5
  677.4 3.3 all-to-all-start
  680.8 5.9 all-to-all-done
  687.3 3.3 all-to-all-start.1
  690.7 5.9 all-to-all-done.1
  697.3 3.3 all-to-all-start.2
  700.7 5.9 all-to-all-done.2
  706.6 9.1 %all_to_all.56 = bf16[8,1,72]{2,1,0:T(2,128)(2,1)} all-to-all(bf16[8,1,72]{2,1,0:T(2,128)(2,1)S(1)} %broadcast_in_dim.146), channel_id=1, replica_groups=mesh['rep'=8,'fsdp'=16] {'rep'}, dimensions={0} | all-to-all | bytes 2304 | tf_op jit(solution)/shard_map/all_to_all | solution.py:41
  717.7 5.2 all-to-all-start.9
  722.9 4.3 reshape.455
  728.1 8.7 %all-to-all-done.9 = bf16[8,64,1152]{2,1,0:T(8,128)(2,1)S(1)} async-done(((bf16[8,64,1152]{2,1,0:T(8,128)(2,1)}), bf16[8,64,1152]{2,1,0:T(8,128)(2,1)S(1)}, u32[]{:S(2)}, u32[]{:S(2)}) %all-to-all-start.9) | async-done | bytes 1179680 | tf_op jit(solution)/shard_map/all_to_all | solution.py:41
  737.5 3.4 all-to-all-start.8
  740.9 5.5 fusion.98
  749.0 4.1 all-to-all-start.7
  754.1 8.1 %all-to-all-done.7 = bf16[8,72,256]{2,1,0:T(8,128)(2,1)} async-done(((bf16[8,72,256]{2,1,0:T(8,128)(2,1)}), bf16[8,72,256]{2,1,0:T(8,128)(2,1)}, u32[]{:S(2)}, u32[]{:S(2)}) %all-to-all-start.7) | async-done | bytes 294944 | tf_op jit(solution)/shard_map/all_to_all | solution.py:41
  763.4 4.3 all-to-all-start.6
  776.7 3.2 all-to-all-done.6
  (295 shorter events, 88.6 us)
Async XLA Ops:
  7.2 183.1 %copy-start = (bf16[432,1152]{1,0:T(8,128)(2,1)S(1)}, bf16[432,1152]{1,0:T(8,128)(2,1)}, u32[]{:S(2)}) copy-start(bf16[432,1152]{1,0:T(8,128)(2,1)} %param.31) | copy-start | bytes 2985988
  7.2 94.9 %copy-start.2 = (bf16[128,1152]{1,0:T(8,128)(2,1)S(1)}, bf16[128,1152]{1,0:T(8,128)(2,1)}, u32[]{:S(2)}) copy-start(bf16[128,1152]{1,0:T(8,128)(2,1)} %param.16) | copy-start | bytes 884740
  7.2 85.4 %all-gather.8.cloned.1.call-start = ((), (), s32[]{:S(2)}) async-start(), calls=%async_computation.14 | async-start | bytes 3760128 | tf_op jit(solution)/shard_map/all_gather | solution.py:18
  9.0 108.9 %all-gather.10.cloned.1.call-start = ((), (), s32[]{:S(2)}) async-start(), calls=%async_computation.15 | async-start | bytes 2506752 | tf_op jit(solution)/shard_map/all_gather | solution.py:132
  9.8 169.4 %all-gather.12.cloned.1.call-start = ((), (), s32[]{:S(2)}) async-start(), calls=%async_computation.16 | async-start | bytes 5013504 | tf_op jit(solution)/shard_map/all_gather | solution.py:188
  15.1 87.6 %copy-start.32 = (f32[128]{0:T(128)}, f32[128]{0:T(128)S(1)}, u32[]{:S(2)}) copy-start(f32[128]{0:T(128)S(1)} %fusion.83) | copy-start | bytes 1540
  15.6 79.8 %copy-start.38 = (f32[128]{0:T(128)}, f32[128]{0:T(128)S(1)}, u32[]{:S(2)}) copy-start(f32[128]{0:T(128)S(1)} %subtract_convert_fusion) | copy-start | bytes 1540
  96.9 12.0 %collective-permute-start.3 = (bf16[128,512]{1,0:T(8,128)(2,1)S(1)}, bf16[128,512]{1,0:T(8,128)(2,1)S(1)}, u32[]{:S(2)}, u32[]{:S(2)}) collective-permute-start(bf16[128,512]{1,0:T(8,128)(2,1)S(1)} %pad_maximum_fusion.4), channel_id=1, source_target_pairs={{0,1},{1,2},{2,3},{3,4},{4,5},{5,6},{6,7},{7,8},{8,9},{9,10},{10,1... | collective-permute-start | bytes 393224 | tf_op jit(solution)/shard_map/ppermute | solution.py:25
  98.2 10.7 %collective-permute-start.2 = (bf16[128,512]{1,0:T(8,128)(2,1)S(1)}, bf16[128,512]{1,0:T(8,128)(2,1)S(1)}, u32[]{:S(2)}, u32[]{:S(2)}) collective-permute-start(bf16[128,512]{1,0:T(8,128)(2,1)S(1)} %pad_maximum_fusion.4), channel_id=1, source_target_pairs={{0,2},{1,3},{2,4},{3,5},{4,6},{5,7},{6,8},{7,9},{8,10},{9,11},{10,... | collective-permute-start | bytes 393224 | tf_op jit(solution)/shard_map/ppermute | solution.py:25
  99.5 9.4 %collective-permute-start.1 = (bf16[128,512]{1,0:T(8,128)(2,1)S(1)}, bf16[128,512]{1,0:T(8,128)(2,1)S(1)}, u32[]{:S(2)}, u32[]{:S(2)}) collective-permute-start(bf16[128,512]{1,0:T(8,128)(2,1)S(1)} %pad_maximum_fusion.4), channel_id=1, source_target_pairs={{0,3},{1,4},{2,5},{3,6},{4,7},{5,8},{6,9},{7,10},{8,11},{9,12},{10... | collective-permute-start | bytes 393224 | tf_op jit(solution)/shard_map/ppermute | solution.py:25
  100.8 6.5 collective-permute-start
  120.2 64.2 %copy-start.48 = (f32[128]{0:T(128)}, f32[128]{0:T(128)S(1)}, u32[]{:S(2)}) copy-start(f32[128]{0:T(128)S(1)} %get-tuple-element.70) | copy-start | bytes 1540
  122.2 153.5 %reduce-scatter.9.cloned.1.call-start = ((), (), s32[]{:S(2)}) async-start(), calls=%async_computation.17 | async-start | bytes 5013504 | tf_op jit(solution)/shard_map/reduce_scatter | solution.py:196
  194.9 81.9 %copy-start.10 = (bf16[128,1152]{1,0:T(8,128)(2,1)S(1)}, bf16[128,1152]{1,0:T(8,128)(2,1)}, u32[]{:S(2)}) copy-start(bf16[128,1152]{1,0:T(8,128)(2,1)} %param.18) | copy-start | bytes 884740
  195.0 142.2 %all-gather.14.cloned.1.call-start = ((), (), s32[]{:S(2)}) async-start(), calls=%async_computation.18 | async-start | bytes 5013504 | tf_op jit(solution)/shard_map/all_gather | solution.py:207
  280.5 153.8 %reduce-scatter.11.cloned.1.call-start = ((), (), s32[]{:S(2)}) async-start(), calls=%async_computation.19 | async-start | bytes 5013504 | tf_op jit(solution)/shard_map/reduce_scatter | solution.py:222
  353.7 362.0 %reduce-scatter.13.cloned.1.call-start = ((), (), s32[]{:S(2)}) async-start(), calls=%async_computation.20 | async-start | bytes 2506752 | tf_op jit(solution)/shard_map/reduce_scatter | solution.py:344
  369.6 66.0 %copy-start.4 = (f32[128,1152]{1,0:T(8,128)S(1)}, f32[128,1152]{1,0:T(8,128)}, u32[]{:S(2)}) copy-start(f32[128,1152]{1,0:T(8,128)} %copy-done.3) | copy-start | bytes 1769476
  369.6 66.0 %copy-start.9 = (bf16[128,1152]{1,0:T(8,128)(2,1)S(1)}, bf16[128,1152]{1,0:T(8,128)(2,1)}, u32[]{:S(2)}) copy-start(bf16[128,1152]{1,0:T(8,128)(2,1)} %reduce-scatter.9.cloned.1.call-done) | copy-start | bytes 884740
  369.6 68.7 %copy-start.49 = (f32[128]{0:T(128)S(1)}, f32[128]{0:T(128)}, u32[]{:S(2)}) copy-start(f32[128]{0:T(128)} %copy-done.48) | copy-start | bytes 1540
  441.4 84.8 %copy-start.47 = (u32[128]{0:T(128)S(1)}, u32[128]{0:T(128)}, u32[]{:S(2)}) copy-start(u32[128]{0:T(128)} %constant.152) | copy-start | bytes 1540
  441.5 281.5 %all-gather.16.cloned.1.call-start = ((), (), s32[]{:S(2)}) async-start(), calls=%async_computation.21 | async-start | bytes 3483648 | tf_op jit(solution)/shard_map/all_gather | solution.py:59
  524.1 10.3 %collective-permute-start.8 = (bf16[64,3456]{1,0:T(8,128)(2,1)S(1)}, bf16[64,3456]{1,0:T(8,128)(2,1)}, u32[]{:S(2)}, u32[]{:S(2)}) collective-permute-start(bf16[64,3456]{1,0:T(8,128)(2,1)S(1)} %fusion), channel_id=1, source_target_pairs={{0,16},{16,32},{32,48},{48,64},{64,80},{80,96},{96,112},{1,17},{17... | collective-permute-start | bytes 1327112
  527.4 7.0 collective-permute-start.9
  539.4 187.8 %reduce-scatter.15.cloned.1.call-start = ((), (), s32[]{:S(2)}) async-start(), calls=%async_computation.22 | async-start | bytes 3760128
  548.2 17.2 %copy-start.39 = (f32[128]{0:T(128)S(1)}, f32[128]{0:T(128)}, u32[]{:S(2)}) copy-start(f32[128]{0:T(128)} %copy-done.38) | copy-start | bytes 1540
  548.2 17.5 %copy-start.12 = (f32[128,256]{1,0:T(8,128)S(1)}, f32[128,256]{1,0:T(8,128)}, u32[]{:S(2)}) copy-start(f32[128,256]{1,0:T(8,128)} %copy-done.11) | copy-start | bytes 393220
  548.2 17.5 %copy-start.35 = (f32[256]{0:T(256)S(1)}, f32[256]{0:T(256)}, u32[]{:S(2)}) copy-start(f32[256]{0:T(256)} %copy-done.34) | copy-start | bytes 3076
  548.2 17.5 %copy-start.43 = (f32[128]{0:T(128)S(1)}, f32[128]{0:T(128)}, u32[]{:S(2)}) copy-start(f32[128]{0:T(128)} %copy-done.42) | copy-start | bytes 1540
  548.2 17.7 %copy-start.55 = (f32[128]{0:T(128)S(1)}, f32[128]{0:T(128)}, u32[]{:S(2)}) copy-start(f32[128]{0:T(128)} %copy-done.54) | copy-start | bytes 1540
  548.3 6.3 collective-permute-start.4
  549.6 8.4 %collective-permute-start.7 = (bf16[128,512]{1,0:T(8,128)(2,1)S(1)}, bf16[128,512]{1,0:T(8,128)(2,1)S(1)}, u32[]{:S(2)}, u32[]{:S(2)}) collective-permute-start(bf16[128,512]{1,0:T(8,128)(2,1)S(1)} %get-tuple-element.48), channel_id=1, source_target_pairs={{4,0},{5,1},{6,2},{7,3},{8,4},{9,5},{10,6},{11,7},{12,8},{13,9},{1... | collective-permute-start | bytes 393224 | tf_op jit(solution)/shard_map/ppermute | solution.py:25
  550.9 12.0 %collective-permute-start.6 = (bf16[128,512]{1,0:T(8,128)(2,1)S(1)}, bf16[128,512]{1,0:T(8,128)(2,1)S(1)}, u32[]{:S(2)}, u32[]{:S(2)}) collective-permute-start(bf16[128,512]{1,0:T(8,128)(2,1)S(1)} %get-tuple-element.49), channel_id=1, source_target_pairs={{3,0},{4,1},{5,2},{6,3},{7,4},{8,5},{9,6},{10,7},{11,8},{12,9},{13... | collective-permute-start | bytes 393224 | tf_op jit(solution)/shard_map/ppermute | solution.py:25
  552.2 13.1 %collective-permute-start.5 = (bf16[128,512]{1,0:T(8,128)(2,1)S(1)}, bf16[128,512]{1,0:T(8,128)(2,1)S(1)}, u32[]{:S(2)}, u32[]{:S(2)}) collective-permute-start(bf16[128,512]{1,0:T(8,128)(2,1)S(1)} %get-tuple-element.50), channel_id=1, source_target_pairs={{2,0},{3,1},{4,2},{5,3},{6,4},{7,5},{8,6},{9,7},{10,8},{11,9},{12,... | collective-permute-start | bytes 393224 | tf_op jit(solution)/shard_map/ppermute | solution.py:25
  655.7 11.2 %all-to-all-start.4 = ((bf16[8,1,16]{2,1,0:T(2,128)(2,1)}), bf16[8,1,16]{2,1,0:T(2,128)(2,1)S(1)}, u32[]{:S(2)}, u32[]{:S(2)}) async-start(bf16[8,1,16]{2,1,0:T(2,128)(2,1)} %broadcast_in_dim.147), calls=%async_computation.6 | async-start | bytes 8192 | tf_op jit(solution)/shard_map/all_to_all | solution.py:41
  667.5 9.3 %all-to-all-start.5 = ((bf16[8,1,16]{2,1,0:T(2,128)(2,1)}), bf16[8,1,16]{2,1,0:T(2,128)(2,1)S(1)}, u32[]{:S(2)}, u32[]{:S(2)}) async-start(bf16[8,1,16]{2,1,0:T(2,128)(2,1)} %broadcast_in_dim.148), calls=%async_computation.7 | async-start | bytes 8192 | tf_op jit(solution)/shard_map/all_to_all | solution.py:41
  677.4 9.3 %all-to-all-start = ((bf16[8,1,72]{2,1,0:T(2,128)(2,1)}), bf16[8,1,72]{2,1,0:T(2,128)(2,1)S(1)}, u32[]{:S(2)}, u32[]{:S(2)}) async-start(bf16[8,1,72]{2,1,0:T(2,128)(2,1)} %broadcast_in_dim.143), calls=%async_computation.2 | async-start | bytes 8192 | tf_op jit(solution)/shard_map/all_to_all | solution.py:41
  686.7 40.5 %copy-start.29 = (bf16[8,1,72]{2,1,0:T(2,128)(2,1)}, bf16[8,1,72]{2,1,0:T(2,128)(2,1)S(1)}, u32[]{:S(2)}) copy-start(bf16[8,1,72]{2,1,0:T(2,128)(2,1)S(1)} %all-to-all-done) | copy-start | bytes 3460
  687.3 9.3 %all-to-all-start.1 = ((bf16[8,1,72]{2,1,0:T(2,128)(2,1)}), bf16[8,1,72]{2,1,0:T(2,128)(2,1)S(1)}, u32[]{:S(2)}, u32[]{:S(2)}) async-start(bf16[8,1,72]{2,1,0:T(2,128)(2,1)} %broadcast_in_dim.144), calls=%async_computation.3 | async-start | bytes 8192 | tf_op jit(solution)/shard_map/all_to_all | solution.py:41
  696.7 30.6 %copy-start.30 = (bf16[8,1,72]{2,1,0:T(2,128)(2,1)}, bf16[8,1,72]{2,1,0:T(2,128)(2,1)S(1)}, u32[]{:S(2)}) copy-start(bf16[8,1,72]{2,1,0:T(2,128)(2,1)S(1)} %all-to-all-done.1) | copy-start | bytes 3460
  697.3 9.3 %all-to-all-start.2 = ((bf16[8,1,72]{2,1,0:T(2,128)(2,1)}), bf16[8,1,72]{2,1,0:T(2,128)(2,1)S(1)}, u32[]{:S(2)}, u32[]{:S(2)}) async-start(bf16[8,1,72]{2,1,0:T(2,128)(2,1)} %broadcast_in_dim.145), calls=%async_computation.4 | async-start | bytes 8192 | tf_op jit(solution)/shard_map/all_to_all | solution.py:41
  706.6 20.7 %copy-start.31 = (bf16[8,1,72]{2,1,0:T(2,128)(2,1)}, bf16[8,1,72]{2,1,0:T(2,128)(2,1)S(1)}, u32[]{:S(2)}) copy-start(bf16[8,1,72]{2,1,0:T(2,128)(2,1)S(1)} %all-to-all-done.2) | copy-start | bytes 3460
  717.7 19.0 %all-to-all-start.9 = ((bf16[8,64,1152]{2,1,0:T(8,128)(2,1)}), bf16[8,64,1152]{2,1,0:T(8,128)(2,1)S(1)}, u32[]{:S(2)}, u32[]{:S(2)}) async-start(bf16[8,64,1152]{2,1,0:T(8,128)(2,1)} %broadcast_in_dim.152), calls=%async_computation.12 | async-start | bytes 2359296 | tf_op jit(solution)/shard_map/all_to_all | solution.py:41
  737.5 10.8 %all-to-all-start.8 = ((bf16[8,72,256]{2,1,0:T(8,128)(2,1)}), bf16[8,72,256]{2,1,0:T(8,128)(2,1)S(1)}, u32[]{:S(2)}, u32[]{:S(2)}) async-start(bf16[8,72,256]{2,1,0:T(8,128)(2,1)} %broadcast_in_dim.151), calls=%async_computation.10 | async-start | bytes 589824 | tf_op jit(solution)/shard_map/all_to_all | solution.py:41
  740.9 21.3 %slice-start = ((bf16[72,1536]{1,0:T(8,128)(2,1)}), bf16[72,1024]{1,0:T(8,128)(2,1)S(1)}, s32[]{:S(2)}) async-start(bf16[72,1536]{1,0:T(8,128)(2,1)} %reduce-scatter.15.cloned.1.call-done), calls=%async_computation.23 | async-start | bytes 294912 | tf_op jit(solution)/shard_map/split | solution.py:35
  749.0 13.2 %all-to-all-start.7 = ((bf16[8,72,256]{2,1,0:T(8,128)(2,1)}), bf16[8,72,256]{2,1,0:T(8,128)(2,1)}, u32[]{:S(2)}, u32[]{:S(2)}) async-start(bf16[8,72,256]{2,1,0:T(8,128)(2,1)} %broadcast_in_dim.150), calls=%async_computation.9 | async-start | bytes 589824 | tf_op jit(solution)/shard_map/all_to_all | solution.py:41
  754.1 28.0 %copy-start.1 = (bf16[432,1152]{1,0:T(8,128)(2,1)S(1)}, bf16[432,1152]{1,0:T(8,128)(2,1)}, u32[]{:S(2)}) copy-start(bf16[432,1152]{1,0:T(8,128)(2,1)} %param.31) | copy-start | bytes 2985988
  763.4 16.5 %all-to-all-start.6 = ((bf16[8,72,1024]{2,1,0:T(8,128)(2,1)}), bf16[8,72,1024]{2,1,0:T(8,128)(2,1)}, u32[]{:S(2)}, u32[]{:S(2)}) async-start(bf16[8,72,1024]{2,1,0:T(8,128)(2,1)} %broadcast_in_dim.149), calls=%async_computation.8 | async-start | bytes 2359296 | tf_op jit(solution)/shard_map/all_to_all | solution.py:41
  (43 other events, 215.4 us)
Sparse Core Ops, SparseCore 0:
  11.1 55.2 all-gather.7
  68.9 49.0 all-gather.9
  122.3 56.8 all-gather.11
  195.1 80.5 reduce-scatter.8
  280.6 56.4 all-gather.13
  353.8 80.5 reduce-scatter.10
  441.6 78.6 reduce-scatter.12
  539.6 69.3 all-gather.15
  613.6 82.5 reduce-scatter.14
where the time goes:
time: 800 us; the launch traced here: 789 us
  waiting for transfers between devices  337 us (42%)
  blocking collectives  232 us (29%)
  matrix products  67.9 us (8%)
  starting transfers between devices  50.1 us (6%)
  local copies, waits for them, and re-layouts  43 us (5%)
  other arithmetic  39.3 us (5%)
  between operations  18.9 us (2%)
    unnamed x3, blocking collectives  223 us
    reduce_scatter x1, waiting for transfers between devices, local(): lax.psum_scatter(jnp.dot(hidden, down_rows, preferred_element_type=jnp.fl...  80.1 us
    reduce_scatter x1, waiting for transfers between devices, local(): lax.psum_scatter((jnp.dot(group_gate_low, gate_rows, preferred_element_ty...  62.9 us
    all_gather x1, waiting for transfers between devices, local(): group_normed = lax.all_gather(normed_two_low, 'fsdp', axis=0, tiled=True)  57 us
    all_gather x1, waiting for transfers between devices, local(): group_grad_down = lax.all_gather(grad_down_low, 'fsdp', axis=0, tiled=True)  56.6 us
    all_to_all x9, waiting for transfers between devices, from_everyone(): return lax.all_to_all(copies, axis, split_axis=0, concat_axis=0, tiled=True)  50.8 us
    all_to_all x9, starting transfers between devices, from_everyone(): return lax.all_to_all(copies, axis, split_axis=0, concat_axis=0, tiled=True)  35.3 us
    unnamed x152, local copies, waits for them, and re-layouts  23 us
  transfers between devices with their start and end apart: 28, of which 20 were waited for; matrix products, arithmetic and copies ran while one was open for 22% of the time, Pallas kernels for 0%

commit v1 on v0

v1 whole, which is shorter than its diff:
```python
import jax
import jax.numpy as jnp
from jax import lax
from jax.sharding import PartitionSpec as P

WINDOW = 512
EPSILON = 1e-06
MASKED = -1e30
CONTRACT_LAST = (((1,), (1,)), ((), ()))
CONTRACT_FIRST = (((0,), (0,)), ((), ()))
F32 = jnp.float32
LOW = jnp.bfloat16
NZ, NH, NC = (4, 2, 2)
PEERS = [(1, 0), (3, 0), (0, 1), (1, 1), (3, 1), (2, 0), (2, 1)]
CHIPS = [(0, 0)] + PEERS
PAIRS = [((0, 0), (0, 1)), ((1, 0), (3, 0)), ((1, 1), (3, 1)), ((2, 0), (2, 1))]


def place(z, h, c):
    return (z % NZ * NH + h % NH) * NC + c % NC


def route(dz, dh, dc):
    return [
        (place(z + dz, h + dh, c + dc), place(z, h, c))
        for z in range(NZ)
        for h in range(NH)
        for c in range(NC)
    ]


def fetch(block, dz, dh, dc=0):
    return lax.ppermute(block, "fsdp", route(dz, dh, dc))


def hand(block, dz, dh, dc=0):
    return fetch(block, -dz, -dh, -dc)


def swap(block):
    return fetch(block, 0, 0, 1)


def gather_chips(block):
    blocks = {(0, 0): block}
    for peer in PEERS:
        blocks[peer] = fetch(block, *peer)
    return blocks


def coordinates():
    me = lax.axis_index("fsdp")
    return (me // (NH * NC), me // NC % NH, me % NC)


def turned(blocks, start):
    twice = jnp.concatenate([blocks, blocks], axis=0)
    return lax.dynamic_slice_in_dim(twice, start, NZ, 0)


def flipped(blocks, amount, axis):
    return jnp.where(amount == 0, blocks, jnp.flip(blocks, axis))


def to_relative(lines):
    z, h, c = coordinates()
    blocks = lines.reshape(NZ, NH, NC, -1, *lines.shape[1:])
    return flipped(flipped(turned(blocks, z), h, 1), c, 2).reshape(lines.shape)


def to_mesh_order(lines):
    z, h, c = coordinates()
    blocks = lines.reshape(NZ, NH, NC, -1, *lines.shape[1:])
    return flipped(flipped(turned(blocks, (NZ - z) % NZ), h, 1), c, 2).reshape(lines.shape)


def in_offset_order(chips):
    mine = jnp.stack([chips[z, h] for z in range(NZ) for h in range(NH)])
    other = swap(mine)
    both = jnp.stack([mine, other], axis=1)
    return both.reshape(NZ * NH * NC, *mine.shape[1:])


def scatter_sum(blocks):
    chips = blocks.reshape(NZ, NH, NC, *blocks.shape[1:])
    away = swap(chips[:, :, 1].astype(LOW))
    both = chips[:, :, 0].astype(F32) + away.astype(F32)
    total = both[0, 0]
    low = both.astype(LOW)
    for z, h in PEERS:
        total = total + hand(low[z, h], z, h).astype(F32)
    return total


def rep_sum(x):
    copies = jnp.broadcast_to(x.astype(LOW), (lax.axis_size("rep"), *x.shape))
    everything = lax.all_to_all(copies, "rep", split_axis=0, concat_axis=0, tiled=True)
    return jnp.sum(everything.astype(F32), axis=0)


def rep_sum_by_parts(x):
    parts = lax.axis_size("rep")
    lines = x.astype(LOW).reshape(parts, -1, x.shape[1])
    arrived = lax.all_to_all(lines, "rep", split_axis=0, concat_axis=0, tiled=True)
    own = jnp.sum(arrived.astype(F32), axis=0).astype(LOW)
    copies = jnp.broadcast_to(own, (parts, *own.shape))
    whole = lax.all_to_all(copies, "rep", split_axis=0, concat_axis=0, tiled=True)
    return whole.reshape(x.shape).astype(F32)


def shifted(block, axis, distance):
    devices = range(lax.axis_size(axis))
    pairs = [(i - distance, i) for i in devices if i - distance in devices]
    return lax.ppermute(block, axis, pairs)


def norm_rows(values, gain):
    return values * lax.rsqrt(jnp.mean(values * values, axis=-1, keepdims=True) + EPSILON) * gain


def rotate(values, position):
    half = values.shape[-1] // 2
    freq = 10000.0 ** (-2.0 * jnp.arange(half, dtype=F32) / values.shape[-1])
    angle = position.astype(F32)[:, None] * freq[None, :]
    cosine = jnp.cos(angle)[:, None, :]
    sine = jnp.sin(angle)[:, None, :]
    first = values[..., :half]
    second = values[..., half:]
    return jnp.concatenate(
        [first * cosine - second * sine, second * cosine + first * sine], axis=-1
    )


def doc_info(lengths, index):
    ends = jnp.cumsum(lengths)
    starts = ends - lengths
    segment = jnp.sum((index[:, None] >= ends[None, :-1]).astype(jnp.int32), axis=1)
    hit = segment[:, None] == jnp.arange(lengths.shape[0], dtype=jnp.int32)[None, :]
    first = jnp.sum(jnp.where(hit, starts[None, :], 0), axis=1)
    segment = jnp.where(index < 0, -1, segment)
    return (segment, index - first)


def activate(gate, upward):
    return jax.nn.gelu(gate, approximate=True) * upward


def dot(a, b, dims=(((1,), (0,)), ((), ()))):
    return lax.dot_general(a, b, dims, preferred_element_type=F32)


def local(
    tokens,
    lengths,
    cotangent,
    pre_attention,
    post_attention,
    pre_forward,
    post_forward,
    query_gain,
    key_gain,
    query_weight,
    key_weight,
    value_weight,
    output_weight,
    gate_rows,
    up_rows,
    down_rows,
):
    rows = tokens.shape[0]
    width = tokens.shape[1]
    head_size = key_weight.shape[1]
    heads = query_weight.shape[1] // head_size
    features = heads * head_size
    span = features + 2 * head_size
    devices = NZ * NH * NC
    own_rows = query_weight.shape[0]
    own_gain = query_gain.shape[0]
    blocks_back = (WINDOW + rows - 1) // rows
    shard = lax.axis_index("fsdp")
    local_index = shard * rows + jnp.arange(rows, dtype=jnp.int32)
    key_index = (shard - blocks_back) * rows + jnp.arange(rows * (blocks_back + 1), dtype=jnp.int32)
    query_seg, query_pos = doc_info(lengths[0], local_index)
    key_seg, key_place = doc_info(lengths[0], key_index)
    distance = local_index[:, None] - key_index[None, :]
    allowed = (query_seg[:, None] == key_seg[None, :]) & (distance >= 0) & (distance < WINDOW)

    gains = jnp.concatenate(
        [pre_attention, post_attention, pre_forward, post_forward, query_gain, key_gain]
    )
    gain_line = jnp.pad(gains[None, :], ((0, 7), (0, span - gains.shape[0])))
    packed = jnp.concatenate(
        [jnp.concatenate([query_weight, key_weight, value_weight], axis=1), gain_line], axis=0
    )
    first_all = in_offset_order(gather_chips(packed))
    weight_in = first_all[:, :own_rows].reshape(width, span)
    weight_out = in_offset_order(gather_chips(output_weight)).reshape(features, width)
    gain_all = to_mesh_order(first_all[:, own_rows, : gains.shape[0]]).astype(F32)
    gain_pre_att, gain_post_att, gain_pre_fwd, gain_post_fwd = (
        gain_all[:, k * own_rows : (k + 1) * own_rows].reshape(width) for k in range(4)
    )
    gain_query, gain_key = (
        gain_all[:, 4 * own_rows + k * own_gain : 4 * own_rows + (k + 1) * own_gain].reshape(
            head_size
        )
        for k in range(2)
    )
    gate_both = jnp.concatenate([gate_rows, swap(gate_rows)], axis=0)
    up_both = jnp.concatenate([up_rows, swap(up_rows)], axis=0)
    down_both = jnp.concatenate([down_rows, swap(down_rows)], axis=0)

    inputs = tokens.astype(F32)
    normed_one, pull_one = jax.vjp(norm_rows, inputs, gain_pre_att)
    normed_low = normed_one.astype(LOW)
    normed_rel = to_relative(normed_low.T.reshape(devices, own_rows, rows)).reshape(width, rows)
    linear = dot(normed_rel, weight_in, CONTRACT_FIRST)
    query_lin = linear[:, :features]
    key_lin = linear[:, features : features + head_size]
    value_low = linear[:, features + head_size :].astype(LOW)

    def query_side(lin, gain):
        return rotate(
            norm_rows(lin.reshape(rows, heads, head_size), gain), query_pos
        ) * head_size ** (-0.5)

    def key_side(lin, gain):
        return rotate(norm_rows(lin[:, None, :], gain), query_pos)[:, 0, :]

    query_value, pull_query = jax.vjp(query_side, query_lin, gain_query)
    key_value, pull_key = jax.vjp(key_side, key_lin, gain_key)
    query_low = query_value.astype(LOW)
    key_low = key_value.astype(LOW)
    outgoing = jnp.concatenate([key_low, value_low], axis=1)
    arrived = []
    for step in range(blocks_back, 0, -1):
        arrived.append(shifted(outgoing, "fsdp", step))
    both = jnp.concatenate(arrived + [outgoing], axis=0)
    keys_all = both[:, :head_size]
    values_all = both[:, head_size:]
    scores = jnp.einsum("thd,kd->htk", query_low, keys_all, preferred_element_type=F32)
    scores = jnp.where(allowed[None], scores, MASKED)
    peak = jnp.max(scores, axis=-1, keepdims=True)
    expo = jnp.exp(scores - peak)
    total = jnp.sum(expo, axis=-1, keepdims=True)
    probs = expo / total
    probs_low = probs.astype(LOW)
    mixed = jnp.einsum("htk,kd->thd", probs_low, values_all, preferred_element_type=F32)
    mixed_low = mixed.reshape(rows, features).astype(LOW)
    mixed_rel = to_relative(mixed_low.T.reshape(devices, -1, rows)).reshape(features, rows)
    projected = dot(mixed_rel, weight_out, CONTRACT_FIRST)
    attended, pull_two = jax.vjp(norm_rows, projected, gain_post_att)
    residual_one = inputs + attended
    normed_two, pull_three = jax.vjp(norm_rows, residual_one, gain_pre_fwd)
    normed_two_low = normed_two.astype(LOW)

    normed_of = gather_chips(normed_two_low)
    acts = []
    partial = {}
    for pair in PAIRS:
        block = jnp.concatenate([normed_of[p] for p in pair], axis=0)
        gate = dot(block, gate_both, CONTRACT_LAST)
        upward = dot(block, up_both, CONTRACT_LAST)
        hidden = activate(gate, upward).astype(LOW)
        down = dot(hidden, down_both)
        acts.append((block, gate, upward, hidden))
        for k, p in enumerate(pair):
            partial[p] = down[k * rows : (k + 1) * rows]
    down_sum = partial[0, 0]
    for p in PEERS:
        down_sum = down_sum + hand(partial[p].astype(LOW), *p).astype(F32)
    fed, pull_four = jax.vjp(norm_rows, down_sum, gain_post_fwd)
    output = (residual_one + fed).astype(LOW)
    grad_out = cotangent.astype(F32)
    grad_down, grad_post_fwd = pull_four(grad_out)
    grad_down_of = gather_chips(grad_down.astype(LOW))
    saved = []
    partial = {}
    for pair, (block, gate, upward, hidden) in zip(PAIRS, acts):
        grad_block = jnp.concatenate([grad_down_of[p] for p in pair], axis=0)
        grad_hidden = dot(grad_block, down_both, CONTRACT_LAST)
        _, pull = jax.vjp(activate, gate, upward)
        grad_gate, grad_up = pull(grad_hidden)
        gate_low, up_low = (grad_gate.astype(LOW), grad_up.astype(LOW))
        back = dot(gate_low, gate_both) + dot(up_low, up_both)
        saved.append((block, grad_block, gate_low, up_low, hidden))
        for k, p in enumerate(pair):
            partial[p] = back[k * rows : (k + 1) * rows]
    grad_normed_two = partial[0, 0]
    for p in PEERS:
        grad_normed_two = grad_normed_two + hand(partial[p].astype(LOW), *p).astype(F32)
    whole = [jnp.concatenate(parts, axis=0) for parts in zip(*saved)]
    group_normed, group_grad, group_gate, group_up, group_hidden = whole
    row_grads = jnp.concatenate(
        [
            dot(group_gate, group_normed, CONTRACT_FIRST),
            dot(group_up, group_normed, CONTRACT_FIRST),
            dot(group_hidden, group_grad, CONTRACT_FIRST),
        ],
        axis=1,
    )
    hidden_rows = gate_rows.shape[0]
    owned_rows = row_grads[:hidden_rows] + swap(row_grads[hidden_rows:].astype(LOW)).astype(F32)
    spare = -hidden_rows % 64
    owned_rows = rep_sum_by_parts(jnp.pad(owned_rows.astype(LOW), ((0, spare), (0, 0))))
    owned_rows = owned_rows[:hidden_rows]

    extra_three, grad_pre_fwd = pull_three(grad_normed_two)
    grad_residual = grad_out + extra_three
    grad_projected, grad_post_att = pull_two(grad_residual)
    grad_proj_low = grad_projected.astype(LOW)
    grad_mixed_rel = dot(weight_out, grad_proj_low, CONTRACT_LAST).astype(LOW)
    grad_mixed_low = to_mesh_order(grad_mixed_rel.reshape(devices, -1, rows))
    grad_mixed_low = grad_mixed_low.reshape(features, rows).T
    grad_output_weight = dot(mixed_rel, grad_proj_low).reshape(devices, -1, width)
    owned_output = rep_sum(scatter_sum(grad_output_weight))
    grad_mixed_heads = grad_mixed_low.reshape(rows, heads, head_size)
    grad_probs = jnp.einsum("thd,kd->htk", grad_mixed_heads, values_all, preferred_element_type=F32)
    inner = jnp.sum(grad_probs * probs, axis=-1, keepdims=True)
    grad_scores = (probs * (grad_probs - inner)).astype(LOW)
    grad_query_low = jnp.einsum(
        "htk,kd->thd", grad_scores, keys_all, preferred_element_type=F32
    ).astype(LOW)
    grad_keys_all = jnp.einsum("htk,thd->kd", grad_scores, query_low, preferred_element_type=F32)
    grad_values_all = jnp.einsum(
        "htk,thd->kd", probs_low, grad_mixed_heads, preferred_element_type=F32
    )
    grad_both = jnp.concatenate([grad_keys_all, grad_values_all], axis=1)
    owned_both = grad_both[blocks_back * rows :]
    for step in range(1, blocks_back + 1):
        piece = grad_both[(blocks_back - step) * rows : (blocks_back - step + 1) * rows]
        owned_both = owned_both + shifted(piece.astype(LOW), "fsdp", -step).astype(F32)
    grad_key_low = owned_both[:, :head_size].astype(LOW)
    grad_value_low = owned_both[:, head_size:].astype(LOW)
    grad_query_lin, grad_query_gain = pull_query(grad_query_low.astype(F32))
    grad_key_lin, grad_key_gain = pull_key(grad_key_low.astype(F32))
    grad_linear = jnp.concatenate(
        [grad_query_lin.astype(LOW), grad_key_lin.astype(LOW), grad_value_low], axis=1
    )
    grad_normed_rel = dot(weight_in, grad_linear, CONTRACT_LAST)
    grad_normed_one = to_mesh_order(grad_normed_rel.reshape(devices, own_rows, rows))
    grad_normed_one = grad_normed_one.reshape(width, rows).T
    extra_one, grad_pre_att = pull_one(grad_normed_one)
    grad_inputs = grad_residual + extra_one
    grad_weight_in = dot(normed_rel, grad_linear).reshape(devices, own_rows, span)
    gain_grads = jnp.concatenate(
        [
            g.reshape(devices, -1)
            for g in (
                grad_pre_att,
                grad_post_att,
                grad_pre_fwd,
                grad_post_fwd,
                grad_query_gain,
                grad_key_gain,
            )
        ],
        axis=1,
    )
    gain_grads = to_relative(gain_grads)[:, None, :]
    gain_grads = jnp.pad(gain_grads, ((0, 0), (0, 7), (0, span - gain_grads.shape[2])))
    owned_in = rep_sum(scatter_sum(jnp.concatenate([grad_weight_in, gain_grads], axis=1)))
    owned_gains = owned_in[own_rows]
    owned_in = owned_in[:own_rows]
    ends = [k * own_rows for k in range(5)] + [4 * own_rows + own_gain, 4 * own_rows + 2 * own_gain]
    return (
        output,
        grad_inputs,
        *(owned_gains[a:b] for a, b in zip(ends[:-1], ends[1:])),
        owned_in[:, :features],
        owned_in[:, features : features + head_size],
        owned_in[:, features + head_size :],
        owned_output,
        owned_rows[:, :width],
        owned_rows[:, width : 2 * width],
        owned_rows[:, 2 * width :],
    )


def solution(mesh):
    tokens, weight, vector = (P(("rep", "fsdp"), None), P("fsdp", None), P("fsdp"))
    return jax.shard_map(
        local,
        mesh=mesh,
        in_specs=(tokens, P("rep", None), tokens) + (vector,) * 6 + (weight,) * 7,
        out_specs=(tokens, tokens) + (vector,) * 6 + (weight,) * 7,
        check_vma=False,
    )
```

time: 800 us -> 559 us (0.70)
  blocking collectives: 232 us -> 0 us
  waiting for transfers between devices: 337 us -> 184 us
  starting transfers between devices: 50.1 us -> 162 us
  local copies, waits for them, and re-layouts: 43 us -> 82.3 us
  between operations: 18.9 us -> 3.13 us
  other arithmetic: 39.3 us -> 53.8 us
    unnamed x3 -> x0, blocking collectives: 223 us -> none
    reduce_scatter x3 -> x0, waiting for transfers between devices: 143 us -> none  [the longest x1 80.1 us: local(): lax.psum_scatter(jnp.dot(hidden, down_rows, preferred_element_type=jnp.fl...]
    ppermute x8 -> x72, starting transfers between devices: 10.6 us -> 145 us  [the longest x64 127 us: fetch(): return lax.ppermute(block, 'fsdp', route(dz, dh, dc))]
    all_gather x5 -> x0, waiting for transfers between devices: 121 us -> none  [the longest x1 57 us: local(): group_normed = lax.all_gather(normed_two_low, 'fsdp', axis=0, tiled=True)]
    ppermute x8 -> x72, waiting for transfers between devices: 16 us -> 123 us  [the longest x64 122 us: fetch(): return lax.ppermute(block, 'fsdp', route(dz, dh, dc))]
    all_to_all x9 -> x4, starting transfers between devices: 35.3 us -> 17.7 us  [the longest x2 10.2 us: rep_sum(): lax.all_to_all(copies, 'rep', split_axis=0, concat_axis=0, tiled=True)]
    concatenate x0 -> x13, local copies, waits for them, and re-layouts: none -> 14 us  [the longest x1 4.1 us: local(): jnp.concatenate([pre_attention, post_attention, pre_forward, post_forward...]
    slice x0 -> x19, local copies, waits for them, and re-layouts: none -> 11.8 us  [the longest x4 2.52 us: local(): partial[p] = down[k * rows:(k + 1) * rows]]
  transfers between devices with their start and end apart: 28 -> 76, of which waited for: 20 -> 27; matrix products, arithmetic and copies ran while one was open for 22% -> 30% of each run, Pallas kernels for 0% -> 0%
where the time goes in v1:
time: 559 us; the launch traced here: 548 us
  waiting for transfers between devices  184 us (33%)
  starting transfers between devices  162 us (29%)
  local copies, waits for them, and re-layouts  82.3 us (15%)
  matrix products  62.7 us (11%)
  other arithmetic  53.8 us (10%)
    ppermute x64, starting transfers between devices, fetch(): return lax.ppermute(block, 'fsdp', route(dz, dh, dc))  127 us
    ppermute x64, waiting for transfers between devices, fetch(): return lax.ppermute(block, 'fsdp', route(dz, dh, dc))  122 us
    dot_general x33, matrix products, dot(): return lax.dot_general(a, b, dims, preferred_element_type=F32)  52.7 us
    all_to_all x2, waiting for transfers between devices, rep_sum(): lax.all_to_all(copies, 'rep', split_axis=0, concat_axis=0, tiled=True)  32.4 us
    unnamed x244, local copies, waits for them, and re-layouts  30.4 us
    all_to_all x1, waiting for transfers between devices, rep_sum_by_parts(): lax.all_to_all(copies, 'rep', split_axis=0, concat_axis=0, tiled=True)  28.4 us
    ppermute x8, starting transfers between devices, shifted(): return lax.ppermute(block, axis, pairs)  18.1 us
  transfers between devices with their start and end apart: 76, of which 27 were waited for; matrix products, arithmetic and copies ran while one was open for 30% of the time, Pallas kernels for 0%

profile of v1, /device:TPU:0, one launch (start us, length us, event | category | flops | bytes accessed | tf_op | source)
XLA Modules:
  0.0 548.4 jit_solution(5344466275406359014)
XLA Ops:
  0.7 6.5 %collective-permute-start.16 = (bf16[64,1152]{1,0:T(8,128)(2,1)}, bf16[64,1152]{1,0:T(8,128)(2,1)S(1)}, u32[]{:S(2)}, u32[]{:S(2)}) collective-permute-start(bf16[64,1152]{1,0:T(8,128)(2,1)} %param.28), channel_id=1, source_target_pairs={{10,0},{11,1},{8,2},{9,3},{14,4},{15,5},{12,6},{13,7},{2,8},{3,9},... | collective-permute-start | bytes 442376 | tf_op jit(solution)/shard_map/ppermute | solution.py:33
  7.2 3.6 collective-permute-start.14
  11.2 3.0 collective-permute-start.12
  16.6 4.1 concatenate.119
  28.0 7.1 %collective-permute-start.4 = (bf16[80,1536]{1,0:T(8,128)(2,1)S(1)}, bf16[80,1536]{1,0:T(8,128)(2,1)S(1)}, u32[]{:S(2)}, u32[]{:S(2)}) collective-permute-start(bf16[80,1536]{1,0:T(8,128)(2,1)S(1)} %fusion.153), channel_id=1, source_target_pairs={{10,0},{11,1},{8,2},{9,3},{14,4},{15,5},{12,6},{13,7},{2,8},{3,9},... | collective-permute-start | bytes 737288 | tf_op jit(solution)/shard_map/ppermute | solution.py:33
  35.3 7.4 %collective-permute-done.17 = bf16[64,1152]{1,0:T(8,128)(2,1)S(1)} collective-permute-done((bf16[64,1152]{1,0:T(8,128)(2,1)S(1)}, bf16[64,1152]{1,0:T(8,128)(2,1)S(1)}, u32[]{:S(2)}, u32[]{:S(2)}) %collective-permute-start.17) | collective-permute-done | bytes 147488 | tf_op jit(solution)/shard_map/ppermute | solution.py:33
  44.1 6.3 %collective-permute-done = bf16[80,1536]{1,0:T(8,128)(2,1)S(1)} collective-permute-done((bf16[80,1536]{1,0:T(8,128)(2,1)S(1)}, bf16[80,1536]{1,0:T(8,128)(2,1)S(1)}, u32[]{:S(2)}, u32[]{:S(2)}) %collective-permute-start) | collective-permute-done | bytes 245792 | tf_op jit(solution)/shard_map/ppermute | solution.py:33
  51.1 8.1 %collective-permute-done.1 = bf16[80,1536]{1,0:T(8,128)(2,1)S(1)} collective-permute-done((bf16[80,1536]{1,0:T(8,128)(2,1)S(1)}, bf16[80,1536]{1,0:T(8,128)(2,1)S(1)}, u32[]{:S(2)}, u32[]{:S(2)}) %collective-permute-start.1) | collective-permute-done | bytes 245792 | tf_op jit(solution)/shard_map/ppermute | solution.py:33
  59.9 7.9 %collective-permute-done.2 = bf16[80,1536]{1,0:T(8,128)(2,1)S(1)} collective-permute-done((bf16[80,1536]{1,0:T(8,128)(2,1)S(1)}, bf16[80,1536]{1,0:T(8,128)(2,1)S(1)}, u32[]{:S(2)}, u32[]{:S(2)}) %collective-permute-start.2) | collective-permute-done | bytes 245792 | tf_op jit(solution)/shard_map/ppermute | solution.py:33
  71.2 6.4 %collective-permute-done.6 = bf16[80,1536]{1,0:T(8,128)(2,1)S(1)} collective-permute-done((bf16[80,1536]{1,0:T(8,128)(2,1)S(1)}, bf16[80,1536]{1,0:T(8,128)(2,1)S(1)}, u32[]{:S(2)}, u32[]{:S(2)}) %collective-permute-start.6) | collective-permute-done | bytes 245792 | tf_op jit(solution)/shard_map/ppermute | solution.py:33
  86.6 2.9 pad_maximum_fusion.2
  102.8 5.8 %collective-permute-start.9 = (bf16[128,512]{1,0:T(8,128)(2,1)}, bf16[128,512]{1,0:T(8,128)(2,1)}, u32[]{:S(2)}, u32[]{:S(2)}) collective-permute-start(bf16[128,512]{1,0:T(8,128)(2,1)} %pad_maximum_fusion.10), channel_id=1, source_target_pairs={{0,3},{1,4},{2,5},{3,6},{4,7},{5,8},{6,9},{7,10},{8,11},{9,12},{10... | collective-permute-start | bytes 393224 | tf_op jit(solution)/shard_map/ppermute | solution.py:114
  134.3 3.9 collective-permute-start.20
  141.7 5.6 %collective-permute-start.34 = (bf16[128,1152]{1,0:T(8,128)(2,1)S(1)}, bf16[128,1152]{1,0:T(8,128)(2,1)S(1)}, u32[]{:S(2)}, u32[]{:S(2)}) collective-permute-start(bf16[128,1152]{1,0:T(8,128)(2,1)S(1)} %get-tuple-element.28), channel_id=1, source_target_pairs={{10,0},{11,1},{8,2},{9,3},{14,4},{15,5},{12,6},{13,7},{2,8},{3,9},... | collective-permute-start | bytes 884744 | tf_op jit(solution)/shard_map/ppermute | solution.py:33
  152.2 3.0 collective-permute-start.29
  155.2 16.5 %collective-permute-done.25 = bf16[128,1152]{1,0:T(8,128)(2,1)S(1)} collective-permute-done((bf16[128,1152]{1,0:T(8,128)(2,1)S(1)}, bf16[128,1152]{1,0:T(8,128)(2,1)S(1)}, u32[]{:S(2)}, u32[]{:S(2)}) %collective-permute-start.25) | collective-permute-done | bytes 294944 | tf_op jit(solution)/shard_map/ppermute | solution.py:33
  176.5 3.7 collective-permute-start.36
  186.5 3.8 collective-permute-start.32
  208.9 3.5 collective-permute-done.28
  223.8 3.5 collective-permute-start.44
  230.7 5.4 collective-permute-done.38
  238.2 8.9 %collective-permute-done.39 = bf16[128,1152]{1,0:T(8,128)(2,1)S(1)} collective-permute-done((bf16[128,1152]{1,0:T(8,128)(2,1)}, bf16[128,1152]{1,0:T(8,128)(2,1)S(1)}, u32[]{:S(2)}, u32[]{:S(2)}) %collective-permute-start.39) | collective-permute-done | bytes 294944 | tf_op jit(solution)/shard_map/ppermute | solution.py:33
  254.1 4.3 fusion.24
  291.9 3.3 collective-permute-start.45
  301.4 7.1 %collective-permute-done.49 = bf16[128,1152]{1,0:T(8,128)(2,1)S(1)} collective-permute-done((bf16[128,1152]{1,0:T(8,128)(2,1)S(1)}, bf16[128,1152]{1,0:T(8,128)(2,1)S(1)}, u32[]{:S(2)}, u32[]{:S(2)}) %collective-permute-start.49) | collective-permute-done | bytes 294944 | tf_op jit(solution)/shard_map/ppermute | solution.py:33
  308.7 3.1 collective-permute-done.46
  322.0 2.9 fusion.142
  350.8 3.9 fusion.124
  357.4 5.0 collective-permute-start.64
  362.4 7.1 %collective-permute-start.70 = (bf16[64,1152]{1,0:T(8,128)(2,1)S(1)}, bf16[64,1152]{1,0:T(8,128)(2,1)S(1)}, u32[]{:S(2)}, u32[]{:S(2)}) collective-permute-start(bf16[64,1152]{1,0:T(8,128)(2,1)S(1)} %get-tuple-element.60), channel_id=1, source_target_pairs={{10,0},{11,1},{8,2},{9,3},{14,4},{15,5},{12,6},{13,7},{2,8},{3,9},... | collective-permute-start | bytes 442376 | tf_op jit(solution)/shard_map/ppermute | solution.py:33
  370.3 3.1 collective-permute-start.68
  377.7 4.3 collective-permute-start.65
  386.7 5.0 all-to-all-start.1
  391.7 4.1 fusion.1
  397.7 10.1 %all-to-all-done.1 = bf16[8,64,1152]{2,1,0:T(8,128)(2,1)S(1)} async-done(((bf16[8,64,1152]{2,1,0:T(8,128)(2,1)}), bf16[8,64,1152]{2,1,0:T(8,128)(2,1)S(1)}, u32[]{:S(2)}, u32[]{:S(2)}) %all-to-all-start.1) | async-done | bytes 1179680 | tf_op jit(solution)/shard_map/all_to_all | solution.py:97
  408.8 3.6 all-to-all-start.2
  412.5 3.4 fusion.211
  417.6 4.1 collective-permute-start.62
  422.3 3.0 collective-permute-start.60
  426.7 5.4 collective-permute-start.58
  432.1 23.5 %collective-permute-done.62 = bf16[80,1536]{1,0:T(8,128)(2,1)S(1)} collective-permute-done((bf16[80,1536]{1,0:T(8,128)(2,1)S(1)}, bf16[80,1536]{1,0:T(8,128)(2,1)S(1)}, u32[]{:S(2)}, u32[]{:S(2)}) %collective-permute-start.62) | collective-permute-done | bytes 245792 | tf_op jit(solution)/shard_map/ppermute | solution.py:33
  460.9 4.9 collective-permute-done.59
  465.7 4.0 collective-permute-done.58
  473.0 5.2 all-to-all-start
  479.5 22.3 %all-to-all-done = bf16[8,80,1536]{2,1,0:T(8,128)(2,1)} async-done(((bf16[8,80,1536]{2,1,0:T(8,128)(2,1)}), bf16[8,80,1536]{2,1,0:T(8,128)(2,1)}, u32[]{:S(2)}, u32[]{:S(2)}) %all-to-all-start) | async-done | bytes 1966112 | tf_op jit(solution)/shard_map/all_to_all | solution.py:97
  501.8 2.9 broadcast_in_dim.122
  504.7 3.8 all-to-all-start.3
  516.2 28.4 %all-to-all-done.3 = bf16[8,56,3456]{2,1,0:T(8,128)(2,1)S(1)} async-done(((bf16[8,56,3456]{2,1,0:T(8,128)(2,1)}), bf16[8,56,3456]{2,1,0:T(8,128)(2,1)S(1)}, u32[]{:S(2)}, u32[]{:S(2)}) %all-to-all-start.3) | async-done | bytes 3096608 | tf_op jit(solution)/shard_map/all_to_all | solution.py:107
  (539 shorter events, 240.3 us)
Async XLA Ops:
  0.7 34.5 %collective-permute-start.16 = (bf16[64,1152]{1,0:T(8,128)(2,1)}, bf16[64,1152]{1,0:T(8,128)(2,1)S(1)}, u32[]{:S(2)}, u32[]{:S(2)}) collective-permute-start(bf16[64,1152]{1,0:T(8,128)(2,1)} %param.28), channel_id=1, source_target_pairs={{10,0},{11,1},{8,2},{9,3},{14,4},{15,5},{12,6},{13,7},{2,8},{3,9},... | collective-permute-start | bytes 442376 | tf_op jit(solution)/shard_map/ppermute | solution.py:33
  7.2 20.8 %collective-permute-start.15 = (bf16[64,1152]{1,0:T(8,128)(2,1)}, bf16[64,1152]{1,0:T(8,128)(2,1)S(1)}, u32[]{:S(2)}, u32[]{:S(2)}) collective-permute-start(bf16[64,1152]{1,0:T(8,128)(2,1)} %param.28), channel_id=1, source_target_pairs={{8,0},{9,1},{10,2},{11,3},{12,4},{13,5},{14,6},{15,7},{0,8},{1,9},... | collective-permute-start | bytes 442376 | tf_op jit(solution)/shard_map/ppermute | solution.py:33
  7.2 20.7 %collective-permute-start.14 = (bf16[64,1152]{1,0:T(8,128)(2,1)}, bf16[64,1152]{1,0:T(8,128)(2,1)S(1)}, u32[]{:S(2)}, u32[]{:S(2)}) collective-permute-start(bf16[64,1152]{1,0:T(8,128)(2,1)} %param.28), channel_id=1, source_target_pairs={{6,0},{7,1},{4,2},{5,3},{10,4},{11,5},{8,6},{9,7},{14,8},{15,9},{1... | collective-permute-start | bytes 442376 | tf_op jit(solution)/shard_map/ppermute | solution.py:33
  10.8 16.9 %collective-permute-start.13 = (bf16[64,1152]{1,0:T(8,128)(2,1)}, bf16[64,1152]{1,0:T(8,128)(2,1)S(1)}, u32[]{:S(2)}, u32[]{:S(2)}) collective-permute-start(bf16[64,1152]{1,0:T(8,128)(2,1)} %param.28), channel_id=1, source_target_pairs={{4,0},{5,1},{6,2},{7,3},{8,4},{9,5},{10,6},{11,7},{12,8},{13,9},{1... | collective-permute-start | bytes 442376 | tf_op jit(solution)/shard_map/ppermute | solution.py:33
  26.0 52.4 %collective-permute-start.18 = (bf16[64,1152]{1,0:T(8,128)(2,1)}, bf16[64,1152]{1,0:T(8,128)(2,1)S(1)}, u32[]{:S(2)}, u32[]{:S(2)}) collective-permute-start(bf16[64,1152]{1,0:T(8,128)(2,1)} %param.28), channel_id=1, source_target_pairs={{14,0},{15,1},{12,2},{13,3},{2,4},{3,5},{0,6},{1,7},{6,8},{7,9},{4... | collective-permute-start | bytes 442376 | tf_op jit(solution)/shard_map/ppermute | solution.py:33
  27.7 15.0 %collective-permute-start.17 = (bf16[64,1152]{1,0:T(8,128)(2,1)S(1)}, bf16[64,1152]{1,0:T(8,128)(2,1)S(1)}, u32[]{:S(2)}, u32[]{:S(2)}) collective-permute-start(bf16[64,1152]{1,0:T(8,128)(2,1)S(1)} %copy-done.62), channel_id=1, source_target_pairs={{12,0},{13,1},{14,2},{15,3},{0,4},{1,5},{2,6},{3,7},{4,8},{5,9},{6... | collective-permute-start | bytes 442376 | tf_op jit(solution)/shard_map/ppermute | solution.py:33
  27.8 42.6 %collective-permute-start.5 = (bf16[80,1536]{1,0:T(8,128)(2,1)S(1)}, bf16[80,1536]{1,0:T(8,128)(2,1)S(1)}, u32[]{:S(2)}, u32[]{:S(2)}) collective-permute-start(bf16[80,1536]{1,0:T(8,128)(2,1)S(1)} %fusion.153), channel_id=1, source_target_pairs={{12,0},{13,1},{14,2},{15,3},{0,4},{1,5},{2,6},{3,7},{4,8},{5,9},{6... | collective-permute-start | bytes 737288 | tf_op jit(solution)/shard_map/ppermute | solution.py:33
  28.0 41.3 %collective-permute-start.4 = (bf16[80,1536]{1,0:T(8,128)(2,1)S(1)}, bf16[80,1536]{1,0:T(8,128)(2,1)S(1)}, u32[]{:S(2)}, u32[]{:S(2)}) collective-permute-start(bf16[80,1536]{1,0:T(8,128)(2,1)S(1)} %fusion.153), channel_id=1, source_target_pairs={{10,0},{11,1},{8,2},{9,3},{14,4},{15,5},{12,6},{13,7},{2,8},{3,9},... | collective-permute-start | bytes 737288 | tf_op jit(solution)/shard_map/ppermute | solution.py:33
  35.1 33.4 %collective-permute-start.3 = (bf16[80,1536]{1,0:T(8,128)(2,1)S(1)}, bf16[80,1536]{1,0:T(8,128)(2,1)S(1)}, u32[]{:S(2)}, u32[]{:S(2)}) collective-permute-start(bf16[80,1536]{1,0:T(8,128)(2,1)S(1)} %fusion.153), channel_id=1, source_target_pairs={{8,0},{9,1},{10,2},{11,3},{12,4},{13,5},{14,6},{15,7},{0,8},{1,9},... | collective-permute-start | bytes 737288 | tf_op jit(solution)/shard_map/ppermute | solution.py:33
  68.6 16.7 %collective-permute-start.21 = (bf16[432,1152]{1,0:T(8,128)(2,1)}, bf16[432,1152]{1,0:T(8,128)(2,1)}, u32[]{:S(2)}, u32[]{:S(2)}) collective-permute-start(bf16[432,1152]{1,0:T(8,128)(2,1)} %param.29), channel_id=1, source_target_pairs={{1,0},{0,1},{3,2},{2,3},{5,4},{4,5},{7,6},{6,7},{9,8},{8,9},{11,10... | collective-permute-start | bytes 2985992 | tf_op jit(solution)/shard_map/ppermute | solution.py:33
  69.3 69.0 %collective-permute-start.22 = (bf16[432,1152]{1,0:T(8,128)(2,1)}, bf16[432,1152]{1,0:T(8,128)(2,1)}, u32[]{:S(2)}, u32[]{:S(2)}) collective-permute-start(bf16[432,1152]{1,0:T(8,128)(2,1)} %param.30), channel_id=1, source_target_pairs={{1,0},{0,1},{3,2},{2,3},{5,4},{4,5},{7,6},{6,7},{9,8},{8,9},{11,10... | collective-permute-start | bytes 2985992 | tf_op jit(solution)/shard_map/ppermute | solution.py:33
  70.5 69.5 %collective-permute-start.23 = (bf16[432,1152]{1,0:T(8,128)(2,1)}, bf16[432,1152]{1,0:T(8,128)(2,1)}, u32[]{:S(2)}, u32[]{:S(2)}) collective-permute-start(bf16[432,1152]{1,0:T(8,128)(2,1)} %param.31), channel_id=1, source_target_pairs={{1,0},{0,1},{3,2},{2,3},{5,4},{4,5},{7,6},{6,7},{9,8},{8,9},{11,10... | collective-permute-start | bytes 2985992 | tf_op jit(solution)/shard_map/ppermute | solution.py:33
  100.2 21.4 %collective-permute-start.11 = (bf16[128,512]{1,0:T(8,128)(2,1)}, bf16[128,512]{1,0:T(8,128)(2,1)}, u32[]{:S(2)}, u32[]{:S(2)}) collective-permute-start(bf16[128,512]{1,0:T(8,128)(2,1)} %pad_maximum_fusion.10), channel_id=1, source_target_pairs={{0,1},{1,2},{2,3},{3,4},{4,5},{5,6},{6,7},{7,8},{8,9},{9,10},{10,1... | collective-permute-start | bytes 393224 | tf_op jit(solution)/shard_map/ppermute | solution.py:114
  102.8 17.1 %collective-permute-start.9 = (bf16[128,512]{1,0:T(8,128)(2,1)}, bf16[128,512]{1,0:T(8,128)(2,1)}, u32[]{:S(2)}, u32[]{:S(2)}) collective-permute-start(bf16[128,512]{1,0:T(8,128)(2,1)} %pad_maximum_fusion.10), channel_id=1, source_target_pairs={{0,3},{1,4},{2,5},{3,6},{4,7},{5,8},{6,9},{7,10},{8,11},{9,12},{10... | collective-permute-start | bytes 393224 | tf_op jit(solution)/shard_map/ppermute | solution.py:114
  134.3 15.2 %collective-permute-start.20 = (bf16[128,1152]{1,0:T(8,128)(2,1)S(1)}, bf16[128,1152]{1,0:T(8,128)(2,1)S(1)}, u32[]{:S(2)}, u32[]{:S(2)}) collective-permute-start(bf16[128,1152]{1,0:T(8,128)(2,1)S(1)} %get-tuple-element.28), channel_id=1, source_target_pairs={{2,0},{3,1},{0,2},{1,3},{6,4},{7,5},{4,6},{5,7},{10,8},{11,9},{8,1... | collective-permute-start | bytes 884744 | tf_op jit(solution)/shard_map/ppermute | solution.py:33
  141.7 30.4 %collective-permute-start.34 = (bf16[128,1152]{1,0:T(8,128)(2,1)S(1)}, bf16[128,1152]{1,0:T(8,128)(2,1)S(1)}, u32[]{:S(2)}, u32[]{:S(2)}) collective-permute-start(bf16[128,1152]{1,0:T(8,128)(2,1)S(1)} %get-tuple-element.28), channel_id=1, source_target_pairs={{10,0},{11,1},{8,2},{9,3},{14,4},{15,5},{12,6},{13,7},{2,8},{3,9},... | collective-permute-start | bytes 884744 | tf_op jit(solution)/shard_map/ppermute | solution.py:33
  147.2 24.7 %collective-permute-start.33 = (bf16[128,1152]{1,0:T(8,128)(2,1)S(1)}, bf16[128,1152]{1,0:T(8,128)(2,1)S(1)}, u32[]{:S(2)}, u32[]{:S(2)}) collective-permute-start(bf16[128,1152]{1,0:T(8,128)(2,1)S(1)} %get-tuple-element.28), channel_id=1, source_target_pairs={{8,0},{9,1},{10,2},{11,3},{12,4},{13,5},{14,6},{15,7},{0,8},{1,9},... | collective-permute-start | bytes 884744 | tf_op jit(solution)/shard_map/ppermute | solution.py:33
  147.2 24.7 %collective-permute-start.30 = (bf16[128,1152]{1,0:T(8,128)(2,1)S(1)}, bf16[128,1152]{1,0:T(8,128)(2,1)S(1)}, u32[]{:S(2)}, u32[]{:S(2)}) collective-permute-start(bf16[128,1152]{1,0:T(8,128)(2,1)S(1)} %get-tuple-element.28), channel_id=1, source_target_pairs={{14,0},{15,1},{12,2},{13,3},{2,4},{3,5},{0,6},{1,7},{6,8},{7,9},{4... | collective-permute-start | bytes 884744 | tf_op jit(solution)/shard_map/ppermute | solution.py:33
  149.5 22.3 %collective-permute-start.25 = (bf16[128,1152]{1,0:T(8,128)(2,1)S(1)}, bf16[128,1152]{1,0:T(8,128)(2,1)S(1)}, u32[]{:S(2)}, u32[]{:S(2)}) collective-permute-start(bf16[128,1152]{1,0:T(8,128)(2,1)S(1)} %get-tuple-element.28), channel_id=1, source_target_pairs={{12,0},{13,1},{14,2},{15,3},{0,4},{1,5},{2,6},{3,7},{4,8},{5,9},{6... | collective-permute-start | bytes 884744 | tf_op jit(solution)/shard_map/ppermute | solution.py:33
  152.2 19.7 %collective-permute-start.29 = (bf16[128,1152]{1,0:T(8,128)(2,1)S(1)}, bf16[128,1152]{1,0:T(8,128)(2,1)S(1)}, u32[]{:S(2)}, u32[]{:S(2)}) collective-permute-start(bf16[128,1152]{1,0:T(8,128)(2,1)S(1)} %get-tuple-element.28), channel_id=1, source_target_pairs={{6,0},{7,1},{4,2},{5,3},{10,4},{11,5},{8,6},{9,7},{14,8},{15,9},{1... | collective-permute-start | bytes 884744 | tf_op jit(solution)/shard_map/ppermute | solution.py:33
  175.6 25.5 %collective-permute-start.35 = (bf16[128,1152]{1,0:T(8,128)(2,1)S(1)}, bf16[128,1152]{1,0:T(8,128)(2,1)S(1)}, u32[]{:S(2)}, u32[]{:S(2)}) collective-permute-start(bf16[128,1152]{1,0:T(8,128)(2,1)S(1)} %get-tuple-element.85), channel_id=1, source_target_pairs={{8,0},{9,1},{10,2},{11,3},{12,4},{13,5},{14,6},{15,7},{0,8},{1,9},... | collective-permute-start | bytes 884744 | tf_op jit(solution)/shard_map/ppermute | solution.py:33
  176.5 27.3 %collective-permute-start.36 = (bf16[128,1152]{1,0:T(8,128)(2,1)S(1)}, bf16[128,1152]{1,0:T(8,128)(2,1)}, u32[]{:S(2)}, u32[]{:S(2)}) collective-permute-start(bf16[128,1152]{1,0:T(8,128)(2,1)S(1)} %get-tuple-element.86), channel_id=1, source_target_pairs={{10,0},{11,1},{8,2},{9,3},{14,4},{15,5},{12,6},{13,7},{2,8},{3,9},... | collective-permute-start | bytes 884744 | tf_op jit(solution)/shard_map/ppermute | solution.py:33
  184.5 22.6 %collective-permute-start.31 = (bf16[128,1152]{1,0:T(8,128)(2,1)}, bf16[128,1152]{1,0:T(8,128)(2,1)}, u32[]{:S(2)}, u32[]{:S(2)}) collective-permute-start(bf16[128,1152]{1,0:T(8,128)(2,1)} %get-tuple-element.83), channel_id=1, source_target_pairs={{14,0},{15,1},{12,2},{13,3},{2,4},{3,5},{0,6},{1,7},{6,8},{7,9},{4... | collective-permute-start | bytes 884744 | tf_op jit(solution)/shard_map/ppermute | solution.py:33
  186.5 20.6 %collective-permute-start.32 = (bf16[128,1152]{1,0:T(8,128)(2,1)}, bf16[128,1152]{1,0:T(8,128)(2,1)}, u32[]{:S(2)}, u32[]{:S(2)}) collective-permute-start(bf16[128,1152]{1,0:T(8,128)(2,1)} %get-tuple-element.84), channel_id=1, source_target_pairs={{6,0},{7,1},{4,2},{5,3},{10,4},{11,5},{8,6},{9,7},{14,8},{15,9},{1... | collective-permute-start | bytes 884744 | tf_op jit(solution)/shard_map/ppermute | solution.py:33
  219.4 16.6 %collective-permute-start.38 = (bf16[128,1152]{1,0:T(8,128)(2,1)}, bf16[128,1152]{1,0:T(8,128)(2,1)}, u32[]{:S(2)}, u32[]{:S(2)}) collective-permute-start(bf16[128,1152]{1,0:T(8,128)(2,1)} %get-tuple-element.30), channel_id=1, source_target_pairs={{4,0},{5,1},{6,2},{7,3},{8,4},{9,5},{10,6},{11,7},{12,8},{13,9},{1... | collective-permute-start | bytes 884744 | tf_op jit(solution)/shard_map/ppermute | solution.py:33
  219.7 32.6 %collective-permute-start.48 = (bf16[128,1152]{1,0:T(8,128)(2,1)}, bf16[128,1152]{1,0:T(8,128)(2,1)}, u32[]{:S(2)}, u32[]{:S(2)}) collective-permute-start(bf16[128,1152]{1,0:T(8,128)(2,1)} %get-tuple-element.30), channel_id=1, source_target_pairs={{10,0},{11,1},{8,2},{9,3},{14,4},{15,5},{12,6},{13,7},{2,8},{3,9},... | collective-permute-start | bytes 884744 | tf_op jit(solution)/shard_map/ppermute | solution.py:33
  222.1 28.5 %collective-permute-start.47 = (bf16[128,1152]{1,0:T(8,128)(2,1)}, bf16[128,1152]{1,0:T(8,128)(2,1)}, u32[]{:S(2)}, u32[]{:S(2)}) collective-permute-start(bf16[128,1152]{1,0:T(8,128)(2,1)} %get-tuple-element.30), channel_id=1, source_target_pairs={{8,0},{9,1},{10,2},{11,3},{12,4},{13,5},{14,6},{15,7},{0,8},{1,9},... | collective-permute-start | bytes 884744 | tf_op jit(solution)/shard_map/ppermute | solution.py:33
  223.8 25.1 %collective-permute-start.44 = (bf16[128,1152]{1,0:T(8,128)(2,1)}, bf16[128,1152]{1,0:T(8,128)(2,1)}, u32[]{:S(2)}, u32[]{:S(2)}) collective-permute-start(bf16[128,1152]{1,0:T(8,128)(2,1)} %get-tuple-element.30), channel_id=1, source_target_pairs={{14,0},{15,1},{12,2},{13,3},{2,4},{3,5},{0,6},{1,7},{6,8},{7,9},{4... | collective-permute-start | bytes 884744 | tf_op jit(solution)/shard_map/ppermute | solution.py:33
  228.8 18.3 %collective-permute-start.39 = (bf16[128,1152]{1,0:T(8,128)(2,1)}, bf16[128,1152]{1,0:T(8,128)(2,1)S(1)}, u32[]{:S(2)}, u32[]{:S(2)}) collective-permute-start(bf16[128,1152]{1,0:T(8,128)(2,1)} %get-tuple-element.30), channel_id=1, source_target_pairs={{12,0},{13,1},{14,2},{15,3},{0,4},{1,5},{2,6},{3,7},{4,8},{5,9},{6... | collective-permute-start | bytes 884744 | tf_op jit(solution)/shard_map/ppermute | solution.py:33
  262.7 29.2 %collective-permute-start.42 = (bf16[128,1152]{1,0:T(8,128)(2,1)S(1)}, bf16[128,1152]{1,0:T(8,128)(2,1)S(1)}, u32[]{:S(2)}, u32[]{:S(2)}) collective-permute-start(bf16[128,1152]{1,0:T(8,128)(2,1)S(1)} %slice.594), channel_id=1, source_target_pairs={{2,0},{3,1},{0,2},{1,3},{6,4},{7,5},{4,6},{5,7},{10,8},{11,9},{8,1... | collective-permute-start | bytes 884744 | tf_op jit(solution)/shard_map/ppermute | solution.py:33
  269.9 25.3 %collective-permute-start.40 = (bf16[128,1152]{1,0:T(8,128)(2,1)S(1)}, bf16[128,1152]{1,0:T(8,128)(2,1)S(1)}, u32[]{:S(2)}, u32[]{:S(2)}) collective-permute-start(bf16[128,1152]{1,0:T(8,128)(2,1)S(1)} %get-tuple-element.75), channel_id=1, source_target_pairs={{12,0},{13,1},{14,2},{15,3},{0,4},{1,5},{2,6},{3,7},{4,8},{5,9},{6... | collective-permute-start | bytes 884744 | tf_op jit(solution)/shard_map/ppermute | solution.py:33
  272.5 28.6 %collective-permute-start.41 = (bf16[128,1152]{1,0:T(8,128)(2,1)}, bf16[128,1152]{1,0:T(8,128)(2,1)}, u32[]{:S(2)}, u32[]{:S(2)}) collective-permute-start(bf16[128,1152]{1,0:T(8,128)(2,1)} %get-tuple-element.76), channel_id=1, source_target_pairs={{4,0},{5,1},{6,2},{7,3},{8,4},{9,5},{10,6},{11,7},{12,8},{13,9},{1... | collective-permute-start | bytes 884744 | tf_op jit(solution)/shard_map/ppermute | solution.py:33
  287.7 20.9 %collective-permute-start.49 = (bf16[128,1152]{1,0:T(8,128)(2,1)S(1)}, bf16[128,1152]{1,0:T(8,128)(2,1)S(1)}, u32[]{:S(2)}, u32[]{:S(2)}) collective-permute-start(bf16[128,1152]{1,0:T(8,128)(2,1)S(1)} %get-tuple-element.79), channel_id=1, source_target_pairs={{8,0},{9,1},{10,2},{11,3},{12,4},{13,5},{14,6},{15,7},{0,8},{1,9},... | collective-permute-start | bytes 884744 | tf_op jit(solution)/shard_map/ppermute | solution.py:33
  289.2 19.3 %collective-permute-start.50 = (bf16[128,1152]{1,0:T(8,128)(2,1)S(1)}, bf16[128,1152]{1,0:T(8,128)(2,1)S(1)}, u32[]{:S(2)}, u32[]{:S(2)}) collective-permute-start(bf16[128,1152]{1,0:T(8,128)(2,1)S(1)} %get-tuple-element.80), channel_id=1, source_target_pairs={{10,0},{11,1},{8,2},{9,3},{14,4},{15,5},{12,6},{13,7},{2,8},{3,9},... | collective-permute-start | bytes 884744 | tf_op jit(solution)/shard_map/ppermute | solution.py:33
  291.9 16.8 %collective-permute-start.45 = (bf16[128,1152]{1,0:T(8,128)(2,1)S(1)}, bf16[128,1152]{1,0:T(8,128)(2,1)S(1)}, u32[]{:S(2)}, u32[]{:S(2)}) collective-permute-start(bf16[128,1152]{1,0:T(8,128)(2,1)S(1)} %get-tuple-element.77), channel_id=1, source_target_pairs={{14,0},{15,1},{12,2},{13,3},{2,4},{3,5},{0,6},{1,7},{6,8},{7,9},{4... | collective-permute-start | bytes 884744 | tf_op jit(solution)/shard_map/ppermute | solution.py:33
  295.9 16.0 %collective-permute-start.46 = (bf16[128,1152]{1,0:T(8,128)(2,1)S(1)}, bf16[128,1152]{1,0:T(8,128)(2,1)S(1)}, u32[]{:S(2)}, u32[]{:S(2)}) collective-permute-start(bf16[128,1152]{1,0:T(8,128)(2,1)S(1)} %get-tuple-element.78), channel_id=1, source_target_pairs={{6,0},{7,1},{4,2},{5,3},{10,4},{11,5},{8,6},{9,7},{14,8},{15,9},{1... | collective-permute-start | bytes 884744 | tf_op jit(solution)/shard_map/ppermute | solution.py:33
  301.1 90.6 %collective-permute-start.71 = (bf16[432,3456]{1,0:T(8,128)(2,1)}, bf16[432,3456]{1,0:T(8,128)(2,1)}, u32[]{:S(2)}, u32[]{:S(2)}) collective-permute-start(bf16[432,3456]{1,0:T(8,128)(2,1)} %slice.593), channel_id=1, source_target_pairs={{1,0},{0,1},{3,2},{2,3},{5,4},{4,5},{7,6},{6,7},{9,8},{8,9},{11,10... | collective-permute-start | bytes 8957960 | tf_op jit(solution)/shard_map/ppermute | solution.py:33
  357.4 16.1 %collective-permute-start.64 = (bf16[64,1152]{1,0:T(8,128)(2,1)S(1)}, bf16[64,1152]{1,0:T(8,128)(2,1)S(1)}, u32[]{:S(2)}, u32[]{:S(2)}) collective-permute-start(bf16[64,1152]{1,0:T(8,128)(2,1)S(1)} %get-tuple-element.59), channel_id=1, source_target_pairs={{12,0},{13,1},{14,2},{15,3},{0,4},{1,5},{2,6},{3,7},{4,8},{5,9},{6... | collective-permute-start | bytes 442376 | tf_op jit(solution)/shard_map/ppermute | solution.py:33
  383.6 28.9 %collective-permute-start.55 = (bf16[4,2,80,1536]{3,2,1,0:T(8,128)(2,1)}, bf16[4,2,80,1536]{3,2,1,0:T(8,128)(2,1)}, u32[]{:S(2)}, u32[]{:S(2)}) collective-permute-start(bf16[4,2,80,1536]{3,2,1,0:T(8,128)(2,1)} %fusion.7), channel_id=1, source_target_pairs={{1,0},{0,1},{3,2},{2,3},{5,4},{4,5},{7,6},{6,7},{9,8},{8,9},{11,10... | collective-permute-start | bytes 5898248 | tf_op jit(solution)/shard_map/ppermute | solution.py:33
  386.7 21.1 %all-to-all-start.1 = ((bf16[8,64,1152]{2,1,0:T(8,128)(2,1)}), bf16[8,64,1152]{2,1,0:T(8,128)(2,1)S(1)}, u32[]{:S(2)}, u32[]{:S(2)}) async-start(bf16[8,64,1152]{2,1,0:T(8,128)(2,1)} %broadcast_in_dim.121), calls=%async_computation.1 | async-start | bytes 2359296 | tf_op jit(solution)/shard_map/all_to_all | solution.py:97
  408.8 61.8 %all-to-all-start.2 = ((bf16[8,56,3456]{2,1,0:T(8,128)(2,1)}), bf16[8,56,3456]{2,1,0:T(8,128)(2,1)S(1)}, u32[]{:S(2)}, u32[]{:S(2)}) async-start(bf16[8,56,3456]{2,1,0:T(8,128)(2,1)} %bitcast.356), calls=%async_computation.2 | async-start | bytes 6193152 | tf_op jit(solution)/shard_map/all_to_all | solution.py:104
  417.6 38.0 %collective-permute-start.62 = (bf16[80,1536]{1,0:T(8,128)(2,1)S(1)}, bf16[80,1536]{1,0:T(8,128)(2,1)S(1)}, u32[]{:S(2)}, u32[]{:S(2)}) collective-permute-start(bf16[80,1536]{1,0:T(8,128)(2,1)S(1)} %get-tuple-element.45), channel_id=1, source_target_pairs={{10,0},{11,1},{8,2},{9,3},{14,4},{15,5},{12,6},{13,7},{2,8},{3,9},... | collective-permute-start | bytes 737288 | tf_op jit(solution)/shard_map/ppermute | solution.py:33
  421.6 36.8 %collective-permute-start.61 = (bf16[80,1536]{1,0:T(8,128)(2,1)S(1)}, bf16[80,1536]{1,0:T(8,128)(2,1)S(1)}, u32[]{:S(2)}, u32[]{:S(2)}) collective-permute-start(bf16[80,1536]{1,0:T(8,128)(2,1)S(1)} %get-tuple-element.46), channel_id=1, source_target_pairs={{8,0},{9,1},{10,2},{11,3},{12,4},{13,5},{14,6},{15,7},{0,8},{1,9},... | collective-permute-start | bytes 737288 | tf_op jit(solution)/shard_map/ppermute | solution.py:33
  422.3 38.6 %collective-permute-start.60 = (bf16[80,1536]{1,0:T(8,128)(2,1)S(1)}, bf16[80,1536]{1,0:T(8,128)(2,1)S(1)}, u32[]{:S(2)}, u32[]{:S(2)}) collective-permute-start(bf16[80,1536]{1,0:T(8,128)(2,1)S(1)} %get-tuple-element.47), channel_id=1, source_target_pairs={{6,0},{7,1},{4,2},{5,3},{10,4},{11,5},{8,6},{9,7},{14,8},{15,9},{1... | collective-permute-start | bytes 737288 | tf_op jit(solution)/shard_map/ppermute | solution.py:33
  425.3 40.4 %collective-permute-start.59 = (bf16[80,1536]{1,0:T(8,128)(2,1)S(1)}, bf16[80,1536]{1,0:T(8,128)(2,1)S(1)}, u32[]{:S(2)}, u32[]{:S(2)}) collective-permute-start(bf16[80,1536]{1,0:T(8,128)(2,1)S(1)} %get-tuple-element.48), channel_id=1, source_target_pairs={{14,0},{15,1},{12,2},{13,3},{2,4},{3,5},{0,6},{1,7},{6,8},{7,9},{4... | collective-permute-start | bytes 737288 | tf_op jit(solution)/shard_map/ppermute | solution.py:33
  426.7 43.0 %collective-permute-start.58 = (bf16[80,1536]{1,0:T(8,128)(2,1)S(1)}, bf16[80,1536]{1,0:T(8,128)(2,1)S(1)}, u32[]{:S(2)}, u32[]{:S(2)}) collective-permute-start(bf16[80,1536]{1,0:T(8,128)(2,1)S(1)} %get-tuple-element.49), channel_id=1, source_target_pairs={{2,0},{3,1},{0,2},{1,3},{6,4},{7,5},{4,6},{5,7},{10,8},{11,9},{8,1... | collective-permute-start | bytes 737288 | tf_op jit(solution)/shard_map/ppermute | solution.py:33
  473.0 28.8 %all-to-all-start = ((bf16[8,80,1536]{2,1,0:T(8,128)(2,1)}), bf16[8,80,1536]{2,1,0:T(8,128)(2,1)}, u32[]{:S(2)}, u32[]{:S(2)}) async-start(bf16[8,80,1536]{2,1,0:T(8,128)(2,1)} %broadcast_in_dim.120), calls=%async_computation | async-start | bytes 3932160 | tf_op jit(solution)/shard_map/all_to_all | solution.py:97
  504.7 39.9 %all-to-all-start.3 = ((bf16[8,56,3456]{2,1,0:T(8,128)(2,1)}), bf16[8,56,3456]{2,1,0:T(8,128)(2,1)S(1)}, u32[]{:S(2)}, u32[]{:S(2)}) async-start(bf16[8,56,3456]{2,1,0:T(8,128)(2,1)} %broadcast_in_dim.122), calls=%async_computation.3 | async-start | bytes 6193152 | tf_op jit(solution)/shard_map/all_to_all | solution.py:107
  (134 other events, 1175.9 us)
